TPU v7x, 32 devices: a whole 2x2x4 slice. The times are simulated.
32 devices in a mesh: pts: 8 (over z, x), comp: 4 (over y, core).
Axes of the slice: x: 2, y: 2, z: 4, core: 2. Of those that a mesh axis runs over, the one named last changes fastest.
Arguments:
- points: bfloat16 [4096, 3072], P(('pts', 'comp')), may hold values from -6 to 6
- candidates: int32 [4096, 4], P(('pts', 'comp')), may hold values from 0 to 7, all different within a row; in each aligned block of 128 rows (0 to 127, 128 to 255, ...) at most 128 rows name the same one
- means: bfloat16 [1024, 3072], P('comp'), may hold values from -0.75 to 0.75
- variances: float32 [1024], P('comp'), may hold values from 0.9 to 1.1
- log_weights: float32 [1024], P('comp'), may hold values from -4 to 4
Outputs:
- loglik: float32 [4096], P(('pts', 'comp'))
- new_means: float32 [4, 256, 3072], P('comp', 'pts')
- new_variances: float32 [4, 256], P('comp', 'pts')
- new_log_weights: float32 [4, 256], P('comp', 'pts')
Inputs may be any that keep to these rules, and one draw needn't show every extreme that they name: `candidates`: each row names 4 different blocks. Among the 128 rows of one device, no block is named by more than 128 rows, and some block is named by exactly 128 rows.
All inputs are finite; a program needn't handle non-finite values.
Results may differ from a plain program's by a relative error of at most 0.0065.
Values may be sent and summed in bfloat16 or wider, within the bound.
A program may use at most 64 MiB of HBM per device.

v0:
```python
import math

import jax
import jax.numpy as jnp
from jax import lax
from jax.sharding import PartitionSpec as P


def on_device(points, candidates, means, variances, log_weights):
    ncomp = lax.axis_size("comp")
    nshare = lax.axis_size("pts")
    rows_here = points.shape[0]
    cands = candidates.shape[1]
    width = points.shape[1]
    owned = means.shape[0]
    block = owned // 2
    nblocks = 2 * ncomp
    slots = 2 * rows_here * cands // nblocks
    flat = candidates.reshape(-1)
    onehot = (flat[:, None] == jnp.arange(nblocks, dtype=jnp.int32)[None, :]).astype(jnp.int32)
    position = jnp.sum((jnp.cumsum(onehot, axis=0) - 1) * onehot, axis=1)
    slot = flat * slots + position
    source_row = jnp.arange(rows_here * cands, dtype=jnp.int32) // cands
    slot_rows = jnp.full((nblocks * slots,), rows_here, jnp.int32).at[slot].set(source_row)
    outgoing = jnp.take(points, slot_rows, axis=0, mode="fill", fill_value=0).reshape(
        ncomp, 2 * slots, width
    )
    arrived = lax.all_to_all(outgoing, "comp", split_axis=0, concat_axis=0, tiled=True).reshape(
        ncomp, 2, slots, width
    )
    mu_blocks = means.reshape(2, block, width)
    inner = jnp.einsum("slcd,lkd->slck", arrived, mu_blocks, preferred_element_type=jnp.float32)
    sq_rows = jnp.einsum("slcd,slcd->slc", arrived, arrived, preferred_element_type=jnp.float32)
    sq_means = jnp.einsum("lkd,lkd->lk", mu_blocks, mu_blocks, preferred_element_type=jnp.float32)
    var_blocks = variances.reshape(2, block)
    const = log_weights.reshape(2, block) - 0.5 * width * jnp.log(2.0 * math.pi * var_blocks)
    logp = const[None, :, None, :] - (
        sq_rows[..., None] - 2.0 * inner + sq_means[None, :, None, :]
    ) / (2.0 * var_blocks[None, :, None, :])
    block_max = jnp.max(logp, axis=3)
    block_sum = jnp.sum(jnp.exp(logp - block_max[..., None]), axis=3)
    back_max, back_sum = (
        lax.all_to_all(
            block_max.reshape(ncomp, 2 * slots), "comp", split_axis=0, concat_axis=0, tiled=True
        ),
        lax.all_to_all(
            block_sum.reshape(ncomp, 2 * slots), "comp", split_axis=0, concat_axis=0, tiled=True
        ),
    )
    pair_max = back_max.reshape(-1)[slot].reshape(rows_here, cands)
    pair_sum = back_sum.reshape(-1)[slot].reshape(rows_here, cands)
    top = jnp.max(pair_max, axis=1)
    loglik = top + jnp.log(jnp.sum(pair_sum * jnp.exp(pair_max - top[:, None]), axis=1))
    slot_totals = jnp.take(loglik, slot_rows, axis=0, mode="fill", fill_value=1e30).reshape(
        ncomp, 2 * slots
    )
    totals = lax.all_to_all(slot_totals, "comp", split_axis=0, concat_axis=0, tiled=True).reshape(
        ncomp, 2, slots
    )
    resp = jnp.exp(logp - totals[..., None])
    counts = jnp.sum(resp, axis=(0, 2)).reshape(owned)
    sqsum = jnp.sum(resp * sq_rows[..., None], axis=(0, 2)).reshape(owned)
    resp_half = resp.astype(jnp.bfloat16)
    wsum = jnp.einsum(
        "slck,slcd->lkd", resp_half, arrived, preferred_element_type=jnp.float32
    ).reshape(owned, width)
    share = owned // nshare
    first_row = lax.axis_index("pts") * share
    wsum_own, counts_own, sqsum_own = (
        lax.psum_scatter(wsum, "pts", scatter_dimension=0, tiled=True),
        lax.psum_scatter(counts, "pts", scatter_dimension=0, tiled=True),
        lax.psum_scatter(sqsum, "pts", scatter_dimension=0, tiled=True),
    )
    mu_old = lax.dynamic_slice_in_dim(means, first_row, share, 0).astype(jnp.float32)
    var_old = lax.dynamic_slice_in_dim(variances, first_row, share, 0)
    new_means = (wsum_own + mu_old) / (counts_own + 1.0)[:, None]
    resid = (
        sqsum_own
        - 2.0 * jnp.sum(new_means * wsum_own, axis=1)
        + counts_own * jnp.sum(new_means * new_means, axis=1)
        + width * var_old
    )
    new_variances = resid / (width * (counts_own + 1.0))
    total_points = rows_here * ncomp * nshare
    new_log_weights = jnp.log((counts_own + 1.0) / float(total_points + owned * ncomp))
    return (
        loglik,
        new_means.reshape(1, share, width),
        new_variances.reshape(1, share),
        new_log_weights.reshape(1, share),
    )


def solution(mesh):
    return jax.shard_map(
        on_device,
        mesh=mesh,
        in_specs=(
            P(("pts", "comp"), None),
            P(("pts", "comp"), None),
            P("comp", None),
            P("comp"),
            P("comp"),
        ),
        out_specs=(P(("pts", "comp")), P("comp", "pts", None), P("comp", "pts"), P("comp", "pts")),
        check_vma=False,
    )
```

profile of v0, /device:TPU:0, one launch (start us, length us, event | category | flops | bytes accessed | tf_op | source)
XLA Modules:
  0.0 232.9 jit_solution(6507364842266048030)
XLA Ops:
  7.2 0.9 copy.25
  8.3 0.7 broadcast_multiply_fusion
  9.0 1.1 reduce-window.6
  10.1 0.2 slice_reduce_fusion
  10.7 2.4 %scatter_custom_fusion = s32[1024]{0:T(1024)S(1)} fusion(s32[512]{0:T(512)S(1)} %bitcast.62, s32[512]{0:T(512)S(1)} %add_select_fusion, s32[]{:T(128)} %constant.40.clone.1), kind=kCustom, calls=%fused_computation.49 | custom fusion | bytes 4100 | tf_op jit(solution)/shard_map/scatter | solution.py:24
  13.2 6.8 %gather_fusion = bf16[1024,3072]{1,0:T(8,128)(2,1)} fusion(bf16[128,3072]{1,0:T(8,128)(2,1)S(1)} %copy-done, s32[1024]{0:T(1024)S(1)} %fusion.30), kind=kCustom, calls=%fused_computation | custom fusion | bytes 12587008 | tf_op jit(solution)/shard_map/jit(_take)/gather | solution.py:25
  20.0 5.9 %broadcast_select_fusion = bf16[4,256,3072]{2,1,0:T(8,128)(2,1)} fusion(bf16[4,256,3072]{2,1,0:T(8,128)(2,1)} %bitcast.53, pred[4,256]{1,0:T(4,128)(4,1)S(1)} %broadcast_in_dim.35), kind=kLoop, calls=%fused_computation.7 | loop fusion | flops 3145728 | bytes 12583936 | tf_op jit(solution)/shard_map/jit(_take)/select_n | solution.py:25
  25.9 5.4 %all-to-all-start = ((bf16[4,256,3072]{2,1,0:T(8,128)(2,1)}), bf16[4,256,3072]{2,1,0:T(8,128)(2,1)}, u32[]{:S(2)}, u32[]{:S(2)}) async-start(bf16[4,256,3072]{2,1,0:T(8,128)(2,1)} %broadcast_select_fusion), calls=%async_computation | async-start | bytes 12582912 | tf_op jit(solution)/shard_map/all_to_all | solution.py:28
  31.3 0.4 fusion.5
  31.7 70.9 %all-to-all-done = bf16[4,256,3072]{2,1,0:T(8,128)(2,1)} async-done(((bf16[4,256,3072]{2,1,0:T(8,128)(2,1)}), bf16[4,256,3072]{2,1,0:T(8,128)(2,1)}, u32[]{:S(2)}, u32[]{:S(2)}) %all-to-all-start) | async-done | bytes 6291488 | tf_op jit(solution)/shard_map/all_to_all | solution.py:28
  102.6 4.1 %fusion = f32[4,2,128]{2,1,0:T(2,128)S(1)} fusion(bf16[4,2,128,3072]{3,2,1,0:T(8,128)(2,1)} %bitcast.6), kind=kLoop, calls=%fused_computation.6 | loop fusion | flops 9436160 | bytes 6295552
  106.7 4.7 %fusion.40 = (f32[4,2,128]{2,0,1:T(4,128)S(1)}, f32[4,2,128,128]{3,2,0,1:T(8,128)S(1)}) fusion(f32[2,128]{1,0:T(2,128)S(1)} %get-tuple-element.14, f32[2,128]{1,0:T(2,128)S(1)} %fusion.5, bf16[2,128,3072,1]{2,1,3,0:T(8,128)(2,1)S(1)} %bitcast.56, bf16[4,2,128,3072]{3,2,1,0:T(8,128)(2,1)} %bitcast.6, f32[4,2,128]{2,0,1:T(4,128)S(1)} %copy.36, ...), kind=kOutput, calls=%fused_computation.64 | convolution fusion | flops 806091776 | bytes 8399872 | tf_op jit(solution)/shard_map/slcd,lkd->slck/dot_general | solution.py:32
  111.4 0.4 exponential_reduce_fusion
  111.8 0.6 copy.29
  112.4 3.2 %all-to-all-start.2 = ((f32[4,1,256]{2,1,0:T(1,128)}), f32[4,1,256]{2,1,0:T(1,128)S(1)}, u32[]{:S(2)}, u32[]{:S(2)}) async-start(f32[4,1,256]{2,1,0:T(1,128)} %copy.29), calls=%async_computation.2 | async-start | bytes 8192 | tf_op jit(solution)/shard_map/all_to_all | solution.py:46
  115.6 0.6 copy.28
  116.2 3.2 %all-to-all-done.2 = f32[4,1,256]{2,1,0:T(1,128)S(1)} async-done(((f32[4,1,256]{2,1,0:T(1,128)}), f32[4,1,256]{2,1,0:T(1,128)S(1)}, u32[]{:S(2)}, u32[]{:S(2)}) %all-to-all-start.2) | async-done | bytes 4128 | tf_op jit(solution)/shard_map/all_to_all | solution.py:46
  119.4 3.2 %all-to-all-start.1 = ((f32[4,1,256]{2,1,0:T(1,128)}), f32[4,1,256]{2,1,0:T(1,128)S(1)}, u32[]{:S(2)}, u32[]{:S(2)}) async-start(f32[4,1,256]{2,1,0:T(1,128)} %copy.28), calls=%async_computation.1 | async-start | bytes 8192 | tf_op jit(solution)/shard_map/all_to_all | solution.py:43
  122.7 2.3 gather_fusion.2
  125.1 1.3 all-to-all-done.1
  126.4 2.3 gather_fusion.1
  128.9 0.2 multiply_reduce_fusion.3
  129.1 6.6 %gather_fusion.3 = f32[1024]{0:T(1024)S(1)} fusion(f32[128]{0:T(128)S(1)} %log_add_fusion, s32[1024]{0:T(1024)S(1)} %fusion.30), kind=kCustom, calls=%fused_computation.3 | custom fusion | bytes 12288 | tf_op jit(solution)/shard_map/jit(_take)/gather | solution.py:54
  135.7 6.1 %all_to_all.29 = f32[4,1,256]{2,1,0:T(1,128)S(1)} all-to-all(f32[4,1,256]{2,1,0:T(1,128)S(1)} %bitcast.61), channel_id=1, replica_groups=mesh['pts'=8,'comp'=4] {'comp'}, dimensions={0} | all-to-all | bytes 8192 | tf_op jit(solution)/shard_map/all_to_all | solution.py:57
  141.8 5.6 %fusion.1 = f32[2,128,3072,1]{2,1,3,0:T(8,128)} fusion(bf16[4,2,128,3072]{3,2,1,0:T(8,128)(2,1)} %bitcast.6, f32[4,2,128,128]{3,2,0,1:T(8,128)S(1)} %get-tuple-element.16, f32[4,2,128]{2,0,1:T(4,128)S(1)} %bitcast.57), kind=kOutput, calls=%fused_computation.8 | convolution fusion | flops 805568512 | bytes 9965568 | tf_op jit(solution)/shard_map/slck,slcd->lkd/dot_general | solution.py:64
  147.5 0.6 dynamic-slice
  148.8 0.4 multiply_reduce_fusion
  149.1 23.0 %all-reduce.2 = (f32[256]{0:T(256)S(1)}, f32[256]{0:T(256)S(1)}) all-reduce(f32[256]{0:T(256)S(1)} %bitcast.66, f32[256]{0:T(256)S(1)} %bitcast.65), channel_id=3, replica_groups=mesh['pts'=8,'comp'=4] {'pts'}, use_global_device_ids=true, to_apply=%region_10.11.clone | all-reduce | flops 512 | bytes 4096
  172.1 0.6 log_bitcast_fusion
  172.7 50.7 %reduce-scatter.2.cloned.1.call-done = f32[32,3072]{1,0:T(8,128)} async-done(((f32[256,3072]{1,0:T(8,128)}), f32[32,3072]{1,0:T(8,128)}) %reduce-scatter.2.cloned.1.call-update) | async-done | bytes 393232 | tf_op jit(solution)/shard_map/reduce_scatter | solution.py:70
  223.4 2.0 multiply_reduce_fusion.2
  225.4 0.6 fusion.38
  (36 shorter events, 1.0 us)
Async XLA Ops:
  7.2 6.0 %copy-start = (bf16[128,3072]{1,0:T(8,128)(2,1)S(1)}, bf16[128,3072]{1,0:T(8,128)(2,1)}, u32[]{:S(2)}) copy-start(bf16[128,3072]{1,0:T(8,128)(2,1)} %param.5) | copy-start | bytes 2359300
  25.9 5.4 %copy-start.2 = (bf16[256,3072]{1,0:T(8,128)(2,1)S(1)}, bf16[256,3072]{1,0:T(8,128)(2,1)}, u32[]{:S(2)}) copy-start(bf16[256,3072]{1,0:T(8,128)(2,1)} %param.7) | copy-start | bytes 4718596
  25.9 5.8 %copy-start.3 = (f32[256]{0:T(256)S(1)}, f32[256]{0:T(256)}, u32[]{:S(2)}) copy-start(f32[256]{0:T(256)} %param.8) | copy-start | bytes 3076
  25.9 5.8 %copy-start.4 = (f32[256]{0:T(256)S(1)}, f32[256]{0:T(256)}, u32[]{:S(2)}) copy-start(f32[256]{0:T(256)} %param.9) | copy-start | bytes 3076
  25.9 76.7 %all-to-all-start = ((bf16[4,256,3072]{2,1,0:T(8,128)(2,1)}), bf16[4,256,3072]{2,1,0:T(8,128)(2,1)}, u32[]{:S(2)}, u32[]{:S(2)}) async-start(bf16[4,256,3072]{2,1,0:T(8,128)(2,1)} %broadcast_select_fusion), calls=%async_computation | async-start | bytes 12582912 | tf_op jit(solution)/shard_map/all_to_all | solution.py:28
  112.4 6.9 %all-to-all-start.2 = ((f32[4,1,256]{2,1,0:T(1,128)}), f32[4,1,256]{2,1,0:T(1,128)S(1)}, u32[]{:S(2)}, u32[]{:S(2)}) async-start(f32[4,1,256]{2,1,0:T(1,128)} %copy.29), calls=%async_computation.2 | async-start | bytes 8192 | tf_op jit(solution)/shard_map/all_to_all | solution.py:46
  119.4 7.0 %all-to-all-start.1 = ((f32[4,1,256]{2,1,0:T(1,128)}), f32[4,1,256]{2,1,0:T(1,128)S(1)}, u32[]{:S(2)}, u32[]{:S(2)}) async-start(f32[4,1,256]{2,1,0:T(1,128)} %copy.28), calls=%async_computation.1 | async-start | bytes 8192 | tf_op jit(solution)/shard_map/all_to_all | solution.py:43
  122.6 100.8 %reduce-scatter.2.cloned.1.call-start = ((), (), s32[]{:S(2)}) async-start(), calls=%async_computation.5 | async-start | bytes 3538944 | tf_op jit(solution)/shard_map/reduce_scatter | solution.py:70
  129.1 18.4 %copy-start.1 = (f32[128]{0:T(128)}, f32[128]{0:T(128)S(1)}, u32[]{:S(2)}) copy-start(f32[128]{0:T(128)S(1)} %log_add_fusion) | copy-start | bytes 1540
  141.8 5.7 %copy-start.5 = (u32[32]{0:T(128)S(1)}, u32[32]{0:T(128)}, u32[]{:S(2)}) copy-start(u32[32]{0:T(128)} %constant.91) | copy-start | bytes 388
Sparse Core Ops, SparseCore 0:
  147.6 75.7 reduce-scatter.1
where the time goes:
time: 233 us
  waiting for transfers between devices  126 us (54%)
  blocking collectives  29.1 us (12%)
  local copies, waits for them, and re-layouts  23.9 us (10%)
  other arithmetic  16.6 us (7%)
  between operations  14.9 us (6%)
  starting transfers between devices  11.8 us (5%)
  matrix products  10.4 us (4%)
    all_to_all x1, waiting for transfers between devices, on_device(): lax.all_to_all(outgoing, 'comp', split_axis=0, concat_axis=0, tiled=True)  70.9 us
    reduce_scatter x1, waiting for transfers between devices, on_device(): lax.psum_scatter(wsum, 'pts', scatter_dimension=0, tiled=True)  50.7 us
    unnamed x1, blocking collectives  23 us
    gather x1, local copies, waits for them, and re-layouts, on_device(): jnp.take(points, slot_rows, axis=0, mode='fill', fill_value=0)  6.78 us
    gather x1, local copies, waits for them, and re-layouts, on_device(): jnp.take(loglik, slot_rows, axis=0, mode='fill', fill_value=1e+30)  6.57 us
    all_to_all x1, blocking collectives, on_device(): lax.all_to_all(slot_totals, 'comp', split_axis=0, concat_axis=0, tiled=True)  6.13 us
    select_n x1, other arithmetic, on_device(): jnp.take(points, slot_rows, axis=0, mode='fill', fill_value=0)  5.93 us
    dot_general x1, matrix products, on_device(): jnp.einsum('slck,slcd->lkd', resp_half, arrived, preferred_element_type=j...  5.65 us
  transfers between devices with their start and end apart: 4, of which 4 were waited for; matrix products, arithmetic and copies ran while one was open for 2% of the time, Pallas kernels for 0%

commit v1 on v0

v1 whole, which is shorter than its diff:
```python
import functools
import math

import jax
import jax.numpy as jnp
from jax import lax
from jax.experimental import pallas as pl
from jax.experimental.pallas import tpu as pltpu
from jax.sharding import PartitionSpec as P

MESH = pl.DeviceIdType.MESH
LANES = 128
LOW = -3.0e38


def em_kernel(
    ncomp, npts, inner, pieces,
    points_ref, cand_ref, means_ref, shares_ref, var_ref, logw_ref,
    loglik_ref, mean_ref, newvar_ref, newlogw_ref,
    gathered, means, mu_old, aux, logp, stats, logliks, resp16, sums,
    wsend, wrecv, relay, wland, wtotal,
    load_sem, y_send, y_recv, sib_send, sib_recv, fwd_send, fwd_recv,
    aux_send, aux_recv, st_send, st_recv, sum_send, sum_recv,
    w_send, w_recv, g_send, g_recv,
):
    here_c, here_p = lax.axis_index("comp"), lax.axis_index("pts")
    ny, ngroups = ncomp // 2, npts // inner
    rows, width = points_ref.shape
    owned = means_ref.shape[0]
    block = owned // 2
    share = owned // npts
    piece = width // pieces
    y, core = here_c // 2, here_c % 2
    other_core = 1 - core
    sibling = y * 2 + other_core
    group, place = here_p // inner, here_p % inner

    load_points = pltpu.make_async_copy(points_ref, gathered.at[here_c], load_sem.at[0])
    load_points.start()
    load_means = pltpu.make_async_copy(means_ref, means, load_sem.at[1])
    load_means.start()
    load_share = pltpu.make_async_copy(shares_ref.at[here_p], mu_old, load_sem.at[2])
    load_share.start()

    barrier = pltpu.get_barrier_semaphore()
    for k in range(1, ncomp):
        pl.semaphore_signal(
            barrier, inc=1, device_id=(here_p, (here_c + k) % ncomp), device_id_type=MESH
        )
    for k in range(1, npts):
        pl.semaphore_signal(
            barrier, inc=1, device_id=((here_p + k) % npts, here_c), device_id_type=MESH
        )
    load_points.wait()
    pl.semaphore_wait(barrier, ncomp + npts - 2)

    sends = []

    def send(src, dst, s_sem, r_sem, device):
        copy = pltpu.make_async_remote_copy(
            src_ref=src, dst_ref=dst, send_sem=s_sem, recv_sem=r_sem,
            device_id=device, device_id_type=MESH,
        )
        copy.start()
        sends.append(copy)

    def arrived(dst, s_sem, r_sem):
        pltpu.make_async_remote_copy(
            src_ref=dst, dst_ref=dst, send_sem=s_sem, recv_sem=r_sem,
            device_id=(here_p, sibling), device_id_type=MESH,
        ).wait_recv()

    def part(slot, c):
        return gathered.at[slot, :, pl.ds(c * piece, piece)]

    for c in range(pieces):
        for k in range(1, ny):
            send(part(here_c, c), part(here_c, c), y_send.at[k - 1, c], y_recv.at[k - 1, c],
                 (here_p, ((y + k) % ny) * 2 + core))
        send(part(here_c, c), part(here_c, c), sib_send.at[c], sib_recv.at[c], (here_p, sibling))

    def add_square(ref):
        def body(j, total):
            x = ref[:, pl.ds(pl.multiple_of(j * LANES, LANES), LANES)].astype(jnp.float32)
            return total + x * x
        return body

    own_points = gathered.at[here_c]
    sq = lax.fori_loop(
        0, width // LANES, add_square(own_points), jnp.zeros((rows, LANES), jnp.float32)
    )
    xx_row = jnp.sum(sq.T, axis=0, keepdims=True)
    ncand = cand_ref.shape[1]
    eye = lax.broadcasted_iota(jnp.int32, (rows, rows), 0) == lax.broadcasted_iota(
        jnp.int32, (rows, rows), 1
    )
    cand = cand_ref[...].astype(jnp.float32)
    cand_rows = [
        jnp.sum(jnp.where(eye, cand[:, j : j + 1], 0.0), axis=0, keepdims=True)
        for j in range(ncand)
    ]
    aux[here_c] = jnp.concatenate(
        cand_rows + [xx_row] + [jnp.zeros((aux.shape[1] - ncand - 1, rows), jnp.float32)], axis=0
    )
    for k in range(1, ncomp):
        send(aux.at[here_c], aux.at[here_c], aux_send.at[k - 1], aux_recv.at[k - 1],
             (here_p, (here_c + k) % ncomp))

    load_means.wait()

    def dot_t(slot, lo, size):
        return lax.dot_general(
            means[:, pl.ds(lo, size)], gathered[slot, :, pl.ds(lo, size)],
            (((1,), (1,)), ((), ())), preferred_element_type=jnp.float32,
        )

    logp[here_c] = dot_t(here_c, 0, width)

    sq = lax.fori_loop(
        0, width // LANES, add_square(means), jnp.zeros((owned, LANES), jnp.float32)
    )
    mm = jnp.sum(sq, axis=1, keepdims=True)
    eye_k = lax.broadcasted_iota(jnp.int32, (owned, owned), 0) == lax.broadcasted_iota(
        jnp.int32, (owned, owned), 1
    )
    var = jnp.sum(jnp.where(eye_k, var_ref[...], 0.0), axis=1, keepdims=True)
    logw = jnp.sum(jnp.where(eye_k, logw_ref[...], 0.0), axis=1, keepdims=True)
    const = logw - 0.5 * width * jnp.log(2.0 * math.pi * var)
    two_var = 2.0 * var

    for c in range(pieces):
        arrived(part(sibling, c), sib_send.at[c], sib_recv.at[c])
    logp[sibling] = dot_t(sibling, 0, width)

    def accumulate(slot, c):
        term = dot_t(slot, c * piece, piece)
        logp[slot] = term if c == 0 else logp[slot] + term

    def take_forwarded(c):
        for k in range(1, ny):
            slot = ((y + ny - k) % ny) * 2 + other_core
            arrived(part(slot, c), fwd_send.at[k - 1, c], fwd_recv.at[k - 1, c])
            accumulate(slot, c)

    for c in range(pieces):
        for k in range(1, ny):
            slot = ((y + ny - k) % ny) * 2 + core
            arrived(part(slot, c), y_send.at[k - 1, c], y_recv.at[k - 1, c])
            send(part(slot, c), part(slot, c), fwd_send.at[k - 1, c], fwd_recv.at[k - 1, c],
                 (here_p, sibling))
            accumulate(slot, c)
        if c:
            take_forwarded(c - 1)
    take_forwarded(pieces - 1)
    for k in range(1, ncomp):
        arrived(aux.at[(here_c + ncomp - k) % ncomp], aux_send.at[k - 1], aux_recv.at[k - 1])

    def named(s, b):
        number = (here_c * 2 + b).astype(jnp.float32)
        hit = aux[s, 0:1, :] == number
        for j in range(1, ncand):
            hit = hit | (aux[s, j : j + 1, :] == number)
        return hit

    for s in range(ncomp):
        xx = aux[s, ncand : ncand + 1, :]
        lp = const - (xx - 2.0 * logp[s] + mm) / two_var
        logp[s] = lp
        tops, totals = [], []
        for b in range(2):
            half = lp[b * block : (b + 1) * block]
            top = jnp.max(half, axis=0, keepdims=True)
            total = jnp.sum(jnp.exp(half - top), axis=0, keepdims=True)
            hit = named(s, b)
            tops.append(jnp.where(hit, top, LOW))
            totals.append(jnp.where(hit, total, 0.0))
        top = jnp.maximum(tops[0], tops[1])
        total = totals[0] * jnp.exp(tops[0] - top) + totals[1] * jnp.exp(tops[1] - top)
        stats[here_c, 0:1, s * rows : (s + 1) * rows] = top
        stats[here_c, 1:2, s * rows : (s + 1) * rows] = total
    for k in range(1, ncomp):
        send(stats.at[here_c], stats.at[here_c], st_send.at[k - 1], st_recv.at[k - 1],
             (here_p, (here_c + k) % ncomp))
    for k in range(1, ncomp):
        arrived(stats.at[(here_c + ncomp - k) % ncomp], st_send.at[k - 1], st_recv.at[k - 1])

    count_sum = [jnp.zeros((block, rows), jnp.float32) for _ in range(2)]
    sq_sum = [jnp.zeros((block, rows), jnp.float32) for _ in range(2)]
    for s in range(ncomp):
        lanes = slice(s * rows, (s + 1) * rows)
        tops = [stats[o, 0:1, lanes] for o in range(ncomp)]
        top = functools.reduce(jnp.maximum, tops)
        total = stats[0, 1:2, lanes] * jnp.exp(tops[0] - top)
        for o in range(1, ncomp):
            total = total + stats[o, 1:2, lanes] * jnp.exp(tops[o] - top)
        loglik = top + jnp.log(total)
        logliks[s] = loglik
        xx = aux[s, ncand : ncand + 1, :]
        for b in range(2):
            resp = jnp.where(
                named(s, b), jnp.exp(logp[s, b * block : (b + 1) * block, :] - loglik), 0.0
            )
            resp16[b * block : (b + 1) * block, lanes] = resp.astype(jnp.bfloat16)
            count_sum[b] = count_sum[b] + resp
            sq_sum[b] = sq_sum[b] + resp * xx
    loglik_ref[...] = logliks[here_c]
    for b in range(2):
        cols = slice(b * block, (b + 1) * block)
        sums[0, 0:1, cols] = jnp.sum(count_sum[b].T, axis=0, keepdims=True)
        sums[0, 1:2, cols] = jnp.sum(sq_sum[b].T, axis=0, keepdims=True)
    for k in range(1, npts):
        send(sums.at[0], sums.at[k], sum_send.at[k - 1], sum_recv.at[k - 1],
             ((here_p + k) % npts, here_c))

    for c in range(pieces):
        cols = pl.ds(c * piece, piece)
        data = gathered[:, :, cols].reshape(ncomp * rows, piece)
        w = jnp.dot(resp16[...], data, preferred_element_type=jnp.float32)
        for g in range(ngroups):
            for i in range(inner):
                first = (g * inner + i) * share
                wsend[i, g, :, cols] = w[first : first + share].astype(jnp.bfloat16)
        for k in range(1, inner):
            to = (place + k) % inner
            send(wsend.at[to, :, :, cols], wrecv.at[k - 1, :, :, cols],
                 w_send.at[k - 1, c], w_recv.at[k - 1, c], (group * inner + to, here_c))

    for c in range(pieces):
        cols = pl.ds(c * piece, piece)
        total = wsend[place, :, :, cols].astype(jnp.float32)
        for k in range(1, inner):
            arrived(wrecv.at[k - 1, :, :, cols], w_send.at[k - 1, c], w_recv.at[k - 1, c])
            total = total + wrecv[k - 1, :, :, cols].astype(jnp.float32)
        wtotal[:, :, cols] = total
        relay[:, :, cols] = total.astype(jnp.bfloat16)
        for k in range(1, ngroups):
            to = (group + k) % ngroups
            send(relay.at[to, :, cols], wland.at[k - 1, :, cols],
                 g_send.at[k - 1, c], g_recv.at[k - 1, c], (to * inner + place, here_c))

    for k in range(1, npts):
        arrived(sums.at[k], sum_send.at[k - 1], sum_recv.at[k - 1])
    both = sums[0]
    for k in range(1, npts):
        both = both + sums[k]
    mine = lax.broadcasted_iota(jnp.int32, (share, owned), 1) == (
        lax.broadcasted_iota(jnp.int32, (share, owned), 0) + here_p * share
    )

    def column(row):
        return jnp.sum(jnp.where(mine, row, 0.0), axis=1, keepdims=True)

    counts, sqsum, var_old = column(both[0:1]), column(both[1:2]), column(var_ref[...])
    load_share.wait()
    cross = jnp.zeros((share, 1), jnp.float32)
    norm = jnp.zeros((share, 1), jnp.float32)
    for c in range(pieces):
        cols = pl.ds(c * piece, piece)
        w = wtotal[group, :, cols]
        for k in range(1, ngroups):
            arrived(wland.at[k - 1, :, cols], g_send.at[k - 1, c], g_recv.at[k - 1, c])
            w = w + wland[k - 1, :, cols].astype(jnp.float32)
        new = (w + mu_old[:, cols].astype(jnp.float32)) / (counts + 1.0)
        mean_ref[:, cols] = new
        cross = cross + jnp.sum(new * w, axis=1, keepdims=True)
        norm = norm + jnp.sum(new * new, axis=1, keepdims=True)
    resid = sqsum - 2.0 * cross + counts * norm + width * var_old
    new_var = resid / (width * (counts + 1.0))
    new_logw = jnp.log((counts + 1.0) / float(rows * ncomp * npts + owned * ncomp))
    eye_s = lax.broadcasted_iota(jnp.int32, (share, share), 0) == lax.broadcasted_iota(
        jnp.int32, (share, share), 1
    )
    newvar_ref[...] = jnp.sum(jnp.where(eye_s, new_var, 0.0), axis=0, keepdims=True)
    newlogw_ref[...] = jnp.sum(jnp.where(eye_s, new_logw, 0.0), axis=0, keepdims=True)

    for copy in sends:
        copy.wait_send()


def on_device(ncomp, npts, points, candidates, means, variances, log_weights):
    rows, width = points.shape
    owned = means.shape[0]
    share = owned // npts
    inner = 2 ** (npts.bit_length() // 2)
    ngroups = npts // inner
    pieces = 4
    ny = ncomp // 2
    aux_rows = -(-(candidates.shape[1] + 1) // 8) * 8
    f32, bf16 = jnp.float32, jnp.bfloat16
    dma = pltpu.SemaphoreType.DMA
    vmem = pl.BlockSpec(memory_space=pltpu.VMEM)
    anywhere = pl.BlockSpec(memory_space=pl.ANY)
    loglik, new_means, new_var, new_logw = pl.pallas_call(
        functools.partial(em_kernel, ncomp, npts, inner, pieces),
        out_shape=(
            jax.ShapeDtypeStruct((1, rows), f32),
            jax.ShapeDtypeStruct((share, width), f32),
            jax.ShapeDtypeStruct((1, share), f32),
            jax.ShapeDtypeStruct((1, share), f32),
        ),
        in_specs=[anywhere, vmem, anywhere, anywhere, vmem, vmem],
        out_specs=(vmem, vmem, vmem, vmem),
        scratch_shapes=[
            pltpu.VMEM((ncomp, rows, width), bf16),
            pltpu.VMEM((owned, width), bf16),
            pltpu.VMEM((share, width), bf16),
            pltpu.VMEM((ncomp, aux_rows, rows), f32),
            pltpu.VMEM((ncomp, owned, rows), f32),
            pltpu.VMEM((ncomp, 2, ncomp * rows), f32),
            pltpu.VMEM((ncomp, 1, rows), f32),
            pltpu.VMEM((owned, ncomp * rows), bf16),
            pltpu.VMEM((npts, 2, owned), f32),
            pltpu.VMEM((inner, ngroups, share, width), bf16),
            pltpu.VMEM((inner - 1, ngroups, share, width), bf16),
            pltpu.VMEM((ngroups, share, width), bf16),
            pltpu.VMEM((ngroups - 1, share, width), bf16),
            pltpu.VMEM((ngroups, share, width), f32),
            dma((3,)),
            dma((ny - 1, pieces)), dma((ny - 1, pieces)),
            dma((pieces,)), dma((pieces,)),
            dma((ny - 1, pieces)), dma((ny - 1, pieces)),
            dma((ncomp - 1,)), dma((ncomp - 1,)),
            dma((ncomp - 1,)), dma((ncomp - 1,)),
            dma((npts - 1,)), dma((npts - 1,)),
            dma((inner - 1, pieces)), dma((inner - 1, pieces)),
            dma((ngroups - 1, pieces)), dma((ngroups - 1, pieces)),
        ],
        compiler_params=pltpu.CompilerParams(
            collective_id=0, has_side_effects=True, vmem_limit_bytes=50 * 1024 * 1024
        ),
        name="em_step",
    )(
        points, candidates, means, means.reshape(npts, share, width),
        variances.reshape(1, owned), log_weights.reshape(1, owned),
    )
    return (
        loglik.reshape(rows),
        new_means.reshape(1, share, width),
        new_var,
        new_logw,
    )


def solution(mesh):
    return jax.shard_map(
        functools.partial(on_device, mesh.shape["comp"], mesh.shape["pts"]),
        mesh=mesh,
        in_specs=(
            P(("pts", "comp"), None),
            P(("pts", "comp"), None),
            P("comp", None),
            P("comp"),
            P("comp"),
        ),
        out_specs=(P(("pts", "comp")), P("comp", "pts", None), P("comp", "pts"), P("comp", "pts")),
        check_vma=False,
    )
```

time: 233 us -> 62.8 us (0.27)
  waiting for transfers between devices: 126 us -> 0 us
  Pallas kernels: 0 us -> 55 us
  blocking collectives: 29.1 us -> 0 us
  local copies, waits for them, and re-layouts: 23.9 us -> 6.96 us
  other arithmetic: 16.6 us -> 0 us
  between operations: 14.9 us -> 0.65 us
  starting transfers between devices: 11.8 us -> 0 us
  matrix products: 10.4 us -> 0 us
    all_to_all x3 -> x0, waiting for transfers between devices: 75.4 us -> none  [the longest x1 70.9 us: on_device(): lax.all_to_all(outgoing, 'comp', split_axis=0, concat_axis=0, tiled=True)]
    pallas_call x0 -> x1, Pallas kernels: none -> 55 us  [on_device(): pl.pallas_call(functools.partial(em_kernel, ncomp, npts, inner, pieces),...]
    reduce_scatter x1 -> x0, waiting for transfers between devices: 50.7 us -> none  [on_device(): lax.psum_scatter(wsum, 'pts', scatter_dimension=0, tiled=True)]
    unnamed x1 -> x0, blocking collectives: 23 us -> none
    gather x4 -> x0, local copies, waits for them, and re-layouts: 17.9 us -> none  [the longest x1 6.78 us: on_device(): jnp.take(points, slot_rows, axis=0, mode='fill', fill_value=0)]
    all_to_all x3 -> x0, starting transfers between devices: 11.8 us -> none  [the longest x1 5.37 us: on_device(): lax.all_to_all(outgoing, 'comp', split_axis=0, concat_axis=0, tiled=True)]
    dot_general x2 -> x0, matrix products: 10.4 us -> none  [the longest x1 5.65 us: on_device(): jnp.einsum('slck,slcd->lkd', resp_half, arrived, preferred_element_type=j...]
    all_to_all x1 -> x0, blocking collectives: 6.13 us -> none  [on_device(): lax.all_to_all(slot_totals, 'comp', split_axis=0, concat_axis=0, tiled=True)]
  transfers between devices with their start and end apart: 4 -> 0, of which waited for: 4 -> 0; matrix products, arithmetic and copies ran while one was open for 2% -> 0% of each run, Pallas kernels for 0% -> 0%
where the time goes in v1:
time: 62.8 us; the launch traced here: 62.6 us
  Pallas kernels  55 us (88%)
  local copies, waits for them, and re-layouts  6.96 us (11%)
  between operations  0.65 us (1%)
    pallas_call x1, Pallas kernels, on_device(): pl.pallas_call(functools.partial(em_kernel, ncomp, npts, inner, pieces),...  55 us
    unnamed x13, local copies, waits for them, and re-layouts  6.96 us

profile of v1, /device:TPU:0, one launch (start us, length us, event | category | flops | bytes accessed | tf_op | source)
XLA Modules:
  0.0 62.6 jit_solution(1415725107478975476)
XLA Ops:
  0.6 0.8 %copy.9.cand_ref = s32[128,4]{1,0:T(8,128)S(1)} copy(s32[128,4]{0,1:T(4,128)} %param.6) | data formatting | bytes 4096 | tf_op args[1]
  1.4 0.0 copy-start
  1.4 1.4 %copy-done = bf16[256,3072]{1,0:T(8,128)(2,1)S(1)} copy-done((bf16[256,3072]{1,0:T(8,128)(2,1)S(1)}, bf16[256,3072]{1,0:T(8,128)(2,1)}, u32[]{:S(2)}) %copy-start) | copy-done | bytes 1572888
  2.8 0.0 copy-start.1
  2.8 1.1 %copy-done.1 = bf16[128,3072]{1,0:T(8,128)(2,1)S(1)} copy-done((bf16[128,3072]{1,0:T(8,128)(2,1)S(1)}, bf16[128,3072]{1,0:T(8,128)(2,1)}, u32[]{:S(2)}) %copy-start.1) | copy-done | bytes 786456
  4.0 0.0 copy-start.2
  4.0 0.7 %copy-done.2 = f32[256]{0:T(256)S(1)} copy-done((f32[256]{0:T(256)S(1)}, f32[256]{0:T(256)}, u32[]{:S(2)}) %copy-start.2) | copy-done | bytes 1048
  4.6 0.0 copy-start.3
  4.6 0.7 %copy-done.3 = f32[256]{0:T(256)S(1)} copy-done((f32[256]{0:T(256)S(1)}, f32[256]{0:T(256)}, u32[]{:S(2)}) %copy-start.3) | copy-done | bytes 1048
  5.3 55.0 %em_step.1 = (f32[1,128]{1,0:T(1,128)S(1)}, f32[32,3072]{1,0:T(8,128)S(1)}, f32[1,32]{1,0:T(1,128)S(1)}, f32[1,32]{1,0:T(1,128)S(1)}) custom-call(bf16[128,3072]{1,0:T(8,128)(2,1)S(1)} %copy-done.1, s32[128,4]{1,0:T(8,128)S(1)} %copy.9.cand_ref, bf16[256,3072]{1,0:T(8,128)(2,1)S(1)} %copy-done, bf16[8,32,3072]{2,1,0:T(8,128)(2,1)S(1)} %bitcast.5, ...), custom_call_target="tpu_custom_call" | custom-call | tf_op jit(solution)/shard_map/em_step/pallas_call | solution.py:293
  60.3 0.5 copy.14
  60.8 0.7 %copy.15 = f32[1,32,3072]{2,1,0:T(8,128)} copy(f32[1,32,3072]{2,1,0:T(8,128)S(1)} %bitcast.6) | data formatting | bytes 786432
  61.6 0.5 copy.16
  62.1 0.5 copy.17
Async XLA Ops:
  1.4 1.4 %copy-start = (bf16[256,3072]{1,0:T(8,128)(2,1)S(1)}, bf16[256,3072]{1,0:T(8,128)(2,1)}, u32[]{:S(2)}) copy-start(bf16[256,3072]{1,0:T(8,128)(2,1)} %means_ref.1) | copy-start | bytes 4718596
  2.8 1.1 %copy-start.1 = (bf16[128,3072]{1,0:T(8,128)(2,1)S(1)}, bf16[128,3072]{1,0:T(8,128)(2,1)}, u32[]{:S(2)}) copy-start(bf16[128,3072]{1,0:T(8,128)(2,1)} %points_ref.1) | copy-start | bytes 2359300
  4.0 0.7 %copy-start.2 = (f32[256]{0:T(256)S(1)}, f32[256]{0:T(256)}, u32[]{:S(2)}) copy-start(f32[256]{0:T(256)} %param.8) | copy-start | bytes 3076
  4.6 0.7 %copy-start.3 = (f32[256]{0:T(256)S(1)}, f32[256]{0:T(256)}, u32[]{:S(2)}) copy-start(f32[256]{0:T(256)} %param.9) | copy-start | bytes 3076

commit v2 on v1

v2 whole, which is shorter than its diff:
```python
import functools
import math

import jax
import jax.numpy as jnp
from jax import lax
from jax.experimental import pallas as pl
from jax.experimental.pallas import tpu as pltpu
from jax.sharding import PartitionSpec as P

MESH = pl.DeviceIdType.MESH
LANES = 128
LOW = -3.0e38


def em_kernel(
    ncomp, npts, pieces,
    points_ref, cand_ref, means_ref, shares_ref, var_ref, logw_ref,
    loglik_ref, mean_ref, newvar_ref, newlogw_ref,
    gathered, means, mu_old, cands, var_row, logw_row, aux, logp, stats, logliks, resp16, sums,
    wsend, land0, kept, relay1, land1, total, relay2, land2,
    load_sem, y_send, y_recv, sib_send, sib_recv, fwd_send, fwd_recv,
    aux_send, aux_recv, st_send, st_recv, sum_send, sum_recv,
    send0, recv0, send1, recv1, send2, recv2,
):
    here_c, here_p = lax.axis_index("comp"), lax.axis_index("pts")
    ny, ngroups = ncomp // 2, npts // 4
    rows, width = points_ref.shape
    owned = means_ref.shape[0]
    block = owned // 2
    share = owned // npts
    piece = width // pieces
    ncand = cand_ref.shape[0]
    y, core = here_c // 2, here_c % 2
    other_core = 1 - core
    sibling = y * 2 + other_core
    group = here_p // 4
    stride0, stride1 = 1 + core, 2 - core
    bit0, bit1 = (here_p // stride0) % 2, (here_p // stride1) % 2
    partner0 = here_p + (1 - 2 * bit0) * stride0
    partner1 = here_p + (1 - 2 * bit1) * stride1

    barrier = pltpu.get_barrier_semaphore()
    for k in range(1, ncomp):
        pl.semaphore_signal(
            barrier, inc=1, device_id=(here_p, (here_c + k) % ncomp), device_id_type=MESH
        )
    for k in range(1, npts):
        pl.semaphore_signal(
            barrier, inc=1, device_id=((here_p + k) % npts, here_c), device_id_type=MESH
        )

    loads = [
        pltpu.make_async_copy(src, dst, load_sem.at[i])
        for i, (src, dst) in enumerate(
            [
                (points_ref, gathered.at[here_c]), (cand_ref, cands), (means_ref, means),
                (var_ref, var_row), (logw_ref, logw_row), (shares_ref.at[here_p], mu_old),
            ]
        )
    ]
    for load in loads:
        load.start()

    def add_square(ref):
        def body(j, acc):
            x = ref[:, pl.ds(pl.multiple_of(j * LANES, LANES), LANES)].astype(jnp.float32)
            return acc + x * x
        return body

    loads[0].wait()
    loads[1].wait()
    sq = lax.fori_loop(
        0, width // LANES, add_square(gathered.at[here_c]), jnp.zeros((rows, LANES), jnp.float32)
    )
    xx_row = jnp.sum(sq.T, axis=0, keepdims=True)
    aux[here_c] = jnp.concatenate(
        [cands[...].astype(jnp.float32), xx_row]
        + [jnp.zeros((aux.shape[1] - ncand - 1, rows), jnp.float32)],
        axis=0,
    )
    pl.semaphore_wait(barrier, ncomp + npts - 2)

    sends = []

    def send(src, dst, s_sem, r_sem, device):
        copy = pltpu.make_async_remote_copy(
            src_ref=src, dst_ref=dst, send_sem=s_sem, recv_sem=r_sem,
            device_id=device, device_id_type=MESH,
        )
        copy.start()
        sends.append(copy)

    def arrived(dst, s_sem, r_sem):
        pltpu.make_async_remote_copy(
            src_ref=dst, dst_ref=dst, send_sem=s_sem, recv_sem=r_sem,
            device_id=(here_p, sibling), device_id_type=MESH,
        ).wait_recv()

    def part(slot, c):
        return gathered.at[slot, :, pl.ds(c * piece, piece)]

    for c in range(pieces):
        for k in range(1, ny):
            send(part(here_c, c), part(here_c, c), y_send.at[k - 1, c], y_recv.at[k - 1, c],
                 (here_p, ((y + k) % ny) * 2 + core))
        if c == 0:
            for k in range(1, ncomp):
                send(aux.at[here_c], aux.at[here_c], aux_send.at[k - 1], aux_recv.at[k - 1],
                     (here_p, (here_c + k) % ncomp))
    send(gathered.at[here_c], gathered.at[here_c], sib_send.at[0], sib_recv.at[0],
         (here_p, sibling))

    for load in loads[2:]:
        load.wait()

    def dot_t(slot, lo, size):
        return lax.dot_general(
            means[:, pl.ds(lo, size)], gathered[slot, :, pl.ds(lo, size)],
            (((1,), (1,)), ((), ())), preferred_element_type=jnp.float32,
        )

    sq = lax.fori_loop(
        0, width // LANES, add_square(means), jnp.zeros((owned, LANES), jnp.float32)
    )
    mm = jnp.sum(sq, axis=1, keepdims=True)
    eye_k = lax.broadcasted_iota(jnp.int32, (owned, owned), 0) == lax.broadcasted_iota(
        jnp.int32, (owned, owned), 1
    )
    var = jnp.sum(jnp.where(eye_k, var_row[...], 0.0), axis=1, keepdims=True)
    logw = jnp.sum(jnp.where(eye_k, logw_row[...], 0.0), axis=1, keepdims=True)
    const = logw - 0.5 * width * jnp.log(2.0 * math.pi * var)
    two_var = 2.0 * var

    def named(s, b):
        number = (here_c * 2 + b).astype(jnp.float32)
        hit = aux[s, 0:1, :] == number
        for j in range(1, ncand):
            hit = hit | (aux[s, j : j + 1, :] == number)
        return hit

    def finish(s, g):
        xx = aux[s, ncand : ncand + 1, :]
        lp = const - (xx - 2.0 * g + mm) / two_var
        logp[s] = lp
        tops, totals = [], []
        for b in range(2):
            half = lp[b * block : (b + 1) * block]
            top = jnp.max(half, axis=0, keepdims=True)
            hit = named(s, b)
            part_sum = jnp.sum(jnp.exp(half - top), axis=0, keepdims=True)
            tops.append(jnp.where(hit, top, LOW))
            totals.append(jnp.where(hit, part_sum, 0.0))
        top = jnp.maximum(tops[0], tops[1])
        stats[here_c, s, 0:1, :] = top
        stats[here_c, s, 1:2, :] = totals[0] * jnp.exp(tops[0] - top) + totals[1] * jnp.exp(
            tops[1] - top
        )
        for k in range(1, ncomp):
            send(stats.at[here_c, s], stats.at[here_c, s], st_send.at[k - 1, s],
                 st_recv.at[k - 1, s], (here_p, (here_c + k) % ncomp))

    finish(here_c, dot_t(here_c, 0, width))
    for k in range(1, ncomp):
        arrived(aux.at[(here_c + ncomp - k) % ncomp], aux_send.at[k - 1], aux_recv.at[k - 1])
    arrived(gathered.at[sibling], sib_send.at[0], sib_recv.at[0])
    finish(sibling, dot_t(sibling, 0, width))

    def accumulate(slot, c):
        g = dot_t(slot, c * piece, piece)
        if c:
            g = logp[slot] + g
        if c < pieces - 1:
            logp[slot] = g
        else:
            finish(slot, g)

    def take_forwarded(c):
        for k in range(1, ny):
            slot = ((y + ny - k) % ny) * 2 + other_core
            arrived(part(slot, c), fwd_send.at[k - 1, c], fwd_recv.at[k - 1, c])
            accumulate(slot, c)

    for c in range(pieces):
        for k in range(1, ny):
            slot = ((y + ny - k) % ny) * 2 + core
            arrived(part(slot, c), y_send.at[k - 1, c], y_recv.at[k - 1, c])
            send(part(slot, c), part(slot, c), fwd_send.at[k - 1, c], fwd_recv.at[k - 1, c],
                 (here_p, sibling))
            accumulate(slot, c)
        if c:
            take_forwarded(c - 1)
    take_forwarded(pieces - 1)

    for k in range(1, ncomp):
        owner = (here_c + ncomp - k) % ncomp
        for s in range(ncomp):
            arrived(stats.at[owner, s], st_send.at[k - 1, s], st_recv.at[k - 1, s])

    count_sum = [jnp.zeros((block, rows), jnp.float32) for _ in range(2)]
    sq_sum = [jnp.zeros((block, rows), jnp.float32) for _ in range(2)]
    for s in range(ncomp):
        lanes = slice(s * rows, (s + 1) * rows)
        tops = [stats[o, s, 0:1, :] for o in range(ncomp)]
        top = functools.reduce(jnp.maximum, tops)
        weight = stats[0, s, 1:2, :] * jnp.exp(tops[0] - top)
        for o in range(1, ncomp):
            weight = weight + stats[o, s, 1:2, :] * jnp.exp(tops[o] - top)
        loglik = top + jnp.log(weight)
        logliks[s] = loglik
        xx = aux[s, ncand : ncand + 1, :]
        for b in range(2):
            resp = jnp.where(
                named(s, b), jnp.exp(logp[s, b * block : (b + 1) * block, :] - loglik), 0.0
            )
            resp16[b * block : (b + 1) * block, lanes] = resp.astype(jnp.bfloat16)
            count_sum[b] = count_sum[b] + resp
            sq_sum[b] = sq_sum[b] + resp * xx

    def make(c):
        cols = pl.ds(c * piece, piece)
        data = gathered[:, :, cols].reshape(ncomp * rows, piece)
        w = jnp.dot(resp16[...], data, preferred_element_type=jnp.float32)
        for g in range(ngroups):
            for hi in range(2):
                for lo in range(2):
                    first = (g * 4 + hi * 2 + lo) * share
                    wsend[lo + core * (hi - lo), hi + core * (lo - hi), g, :, cols] = w[
                        first : first + share
                    ].astype(jnp.bfloat16)
        send(wsend.at[1 - bit0, :, :, :, cols], land0.at[:, :, :, cols],
             send0.at[c], recv0.at[c], (partner0, here_c))

    def halve(c):
        cols = pl.ds(c * piece, piece)
        arrived(land0.at[:, :, :, cols], send0.at[c], recv0.at[c])
        relay1[:, :, cols] = (
            wsend[bit0, 1 - bit1, :, :, cols].astype(jnp.float32)
            + land0[1 - bit1, :, :, cols].astype(jnp.float32)
        ).astype(jnp.bfloat16)
        send(relay1.at[:, :, cols], land1.at[:, :, cols], send1.at[c], recv1.at[c],
             (partner1, here_c))
        kept[:, :, cols] = wsend[bit0, bit1, :, :, cols].astype(jnp.float32) + land0[
            bit1, :, :, cols
        ].astype(jnp.float32)

    def spread(c):
        cols = pl.ds(c * piece, piece)
        arrived(land1.at[:, :, cols], send1.at[c], recv1.at[c])
        both = kept[:, :, cols] + land1[:, :, cols].astype(jnp.float32)
        relay2[:, :, cols] = both.astype(jnp.bfloat16)
        for k in range(1, ngroups):
            to = (group + k) % ngroups
            send(relay2.at[to, :, cols], land2.at[k - 1, :, cols],
                 send2.at[k - 1, c], recv2.at[k - 1, c], (to * 4 + here_p % 4, here_c))
        total[:, :, cols] = both

    def share_sums():
        loglik_ref[...] = logliks[here_c]
        for b in range(2):
            cols = slice(b * block, (b + 1) * block)
            sums[0, 0:1, cols] = jnp.sum(count_sum[b].T, axis=0, keepdims=True)
            sums[0, 1:2, cols] = jnp.sum(sq_sum[b].T, axis=0, keepdims=True)
        for k in range(1, npts):
            send(sums.at[0], sums.at[k], sum_send.at[k - 1], sum_recv.at[k - 1],
                 ((here_p + k) % npts, here_c))

    def column(row):
        mine = lax.broadcasted_iota(jnp.int32, (share, owned), 1) == (
            lax.broadcasted_iota(jnp.int32, (share, owned), 0) + here_p * share
        )
        return jnp.sum(jnp.where(mine, row, 0.0), axis=1, keepdims=True)

    def take_sums():
        for k in range(1, npts):
            arrived(sums.at[k], sum_send.at[k - 1], sum_recv.at[k - 1])
        both = sums[0]
        for k in range(1, npts):
            both = both + sums[k]
        return column(both[0:1]), column(both[1:2])

    lag = 2
    for t in range(pieces + lag + 2):
        if t < pieces:
            make(t)
        if t == 1:
            share_sums()
        if lag <= t < pieces + lag:
            halve(t - lag)
        if lag < t <= pieces + lag:
            spread(t - lag - 1)
        if t == pieces:
            counts, sqsum = take_sums()
            scale = 1.0 / (counts + 1.0)
            var_old = column(var_row[...])
            cross = jnp.zeros((share, 1), jnp.float32)
            norm = jnp.zeros((share, 1), jnp.float32)
        if t >= pieces:
            ready = [t - lag - 2] if t > pieces else list(range(pieces - lag - 1))
            for c in ready:
                cols = pl.ds(c * piece, piece)
                w = total[group, :, cols]
                for k in range(1, ngroups):
                    arrived(land2.at[k - 1, :, cols], send2.at[k - 1, c], recv2.at[k - 1, c])
                    w = w + land2[k - 1, :, cols].astype(jnp.float32)
                new = (w + mu_old[:, cols].astype(jnp.float32)) * scale
                mean_ref[:, cols] = new
                cross = cross + jnp.sum(new * w, axis=1, keepdims=True)
                norm = norm + jnp.sum(new * new, axis=1, keepdims=True)
    resid = sqsum - 2.0 * cross + counts * norm + width * var_old
    new_var = resid / (width * (counts + 1.0))
    new_logw = jnp.log((counts + 1.0) / float(rows * ncomp * npts + owned * ncomp))
    eye_s = lax.broadcasted_iota(jnp.int32, (share, share), 0) == lax.broadcasted_iota(
        jnp.int32, (share, share), 1
    )
    newvar_ref[...] = jnp.sum(jnp.where(eye_s, new_var, 0.0), axis=0, keepdims=True)
    newlogw_ref[...] = jnp.sum(jnp.where(eye_s, new_logw, 0.0), axis=0, keepdims=True)

    for copy in sends:
        copy.wait_send()


def copy_kernel(*refs):
    count = len(refs) // 2
    copies = [
        pltpu.make_async_copy(refs[i], refs[count + i], refs[-1].at[i]) for i in range(count)
    ]
    for copy in copies:
        copy.start()
    for copy in copies:
        copy.wait()


def on_device(ncomp, npts, points, candidates, means, variances, log_weights):
    rows, width = points.shape
    owned = means.shape[0]
    share = owned // npts
    ngroups = npts // 4
    pieces = 8
    ncand = candidates.shape[1]
    ny = ncomp // 2
    aux_rows = -(-(ncand + 1) // 8) * 8
    f32, bf16 = jnp.float32, jnp.bfloat16
    dma = pltpu.SemaphoreType.DMA
    vmem = pl.BlockSpec(memory_space=pltpu.VMEM)
    anywhere = pl.BlockSpec(memory_space=pl.ANY)
    results = pl.pallas_call(
        functools.partial(em_kernel, ncomp, npts, pieces),
        out_shape=(
            jax.ShapeDtypeStruct((1, rows), f32),
            jax.ShapeDtypeStruct((share, width), f32),
            jax.ShapeDtypeStruct((1, share), f32),
            jax.ShapeDtypeStruct((1, share), f32),
        ),
        in_specs=[anywhere] * 6,
        out_specs=(vmem, vmem, vmem, vmem),
        scratch_shapes=[
            pltpu.VMEM((ncomp, rows, width), bf16),
            pltpu.VMEM((owned, width), bf16),
            pltpu.VMEM((share, width), bf16),
            pltpu.VMEM((ncand, rows), jnp.int32),
            pltpu.VMEM((1, owned), f32),
            pltpu.VMEM((1, owned), f32),
            pltpu.VMEM((ncomp, aux_rows, rows), f32),
            pltpu.VMEM((ncomp, owned, rows), f32),
            pltpu.VMEM((ncomp, ncomp, 2, rows), f32),
            pltpu.VMEM((ncomp, 1, rows), f32),
            pltpu.VMEM((owned, ncomp * rows), bf16),
            pltpu.VMEM((npts, 2, owned), f32),
            pltpu.VMEM((2, 2, ngroups, share, width), bf16),
            pltpu.VMEM((2, ngroups, share, width), bf16),
            pltpu.VMEM((ngroups, share, width), f32),
            pltpu.VMEM((ngroups, share, width), bf16),
            pltpu.VMEM((ngroups, share, width), bf16),
            pltpu.VMEM((ngroups, share, width), f32),
            pltpu.VMEM((ngroups, share, width), bf16),
            pltpu.VMEM((ngroups - 1, share, width), bf16),
            dma((6,)),
            dma((ny - 1, pieces)), dma((ny - 1, pieces)),
            dma((1,)), dma((1,)),
            dma((ny - 1, pieces)), dma((ny - 1, pieces)),
            dma((ncomp - 1,)), dma((ncomp - 1,)),
            dma((ncomp - 1, ncomp)), dma((ncomp - 1, ncomp)),
            dma((npts - 1,)), dma((npts - 1,)),
            dma((pieces,)), dma((pieces,)),
            dma((pieces,)), dma((pieces,)),
            dma((ngroups - 1, pieces)), dma((ngroups - 1, pieces)),
        ],
        compiler_params=pltpu.CompilerParams(
            collective_id=0, has_side_effects=True, vmem_limit_bytes=60 * 1024 * 1024
        ),
        name="em_step",
    )(
        points, candidates.T, means, means.reshape(npts, share, width),
        variances.reshape(1, owned), log_weights.reshape(1, owned),
    )
    loglik, new_means, new_var, new_logw = pl.pallas_call(
        copy_kernel,
        out_shape=tuple(jax.ShapeDtypeStruct(x.shape, x.dtype) for x in results),
        in_specs=[anywhere] * len(results),
        out_specs=(anywhere,) * len(results),
        scratch_shapes=[dma((len(results),))],
        compiler_params=pltpu.CompilerParams(vmem_limit_bytes=60 * 1024 * 1024),
        name="write_results",
    )(*results)
    return (
        loglik.reshape(rows),
        new_means.reshape(1, share, width),
        new_var,
        new_logw,
    )


def solution(mesh):
    return jax.shard_map(
        functools.partial(on_device, mesh.shape["comp"], mesh.shape["pts"]),
        mesh=mesh,
        in_specs=(
            P(("pts", "comp"), None),
            P(("pts", "comp"), None),
            P("comp", None),
            P("comp"),
            P("comp"),
        ),
        out_specs=(P(("pts", "comp")), P("comp", "pts", None), P("comp", "pts"), P("comp", "pts")),
        check_vma=False,
    )
```

time: 62.8 us -> 69.8 us (1.11)
  Pallas kernels: 55 us -> 69 us
  local copies, waits for them, and re-layouts: 6.96 us -> 0 us
    pallas_call x1 -> x2, Pallas kernels: 55 us -> 69 us  [the longest x1 55.9 us: on_device(): pl.pallas_call(functools.partial(em_kernel, ncomp, npts, pieces), out_sha...]
    unnamed x13 -> x0, local copies, waits for them, and re-layouts: 6.96 us -> none
where the time goes in v2:
time: 69.8 us; the launch traced here: 69.7 us
  Pallas kernels  69 us (99%)
    pallas_call x1, Pallas kernels, on_device(): pl.pallas_call(functools.partial(em_kernel, ncomp, npts, pieces), out_sha...  55.9 us
    pallas_call x1, Pallas kernels, on_device(): pl.pallas_call(copy_kernel, out_shape=tuple((jax.ShapeDtypeStruct(x.shape...  13.1 us

profile of v2, /device:TPU:0, one launch (start us, length us, event | category | flops | bytes accessed | tf_op | source)
XLA Modules:
  0.0 69.7 jit_solution(17771741909129196077)
XLA Ops:
  0.6 55.9 %em_step.1 = (f32[1,128]{1,0:T(1,128)}, f32[32,3072]{1,0:T(8,128)}, f32[1,32]{1,0:T(1,128)}, f32[1,32]{1,0:T(1,128)}) custom-call(bf16[128,3072]{1,0:T(8,128)(2,1)} %points_ref.1, s32[4,128]{1,0:T(4,128)} %bitcast.7, bf16[256,3072]{1,0:T(8,128)(2,1)} %means_ref.1, bf16[8,32,3072]{2,1,0:T(8,128)(2,1)} %bitcast.6, f32[1,256]{1,0:T(1,128)} %bitcast.8, ...), custom_call_target="tpu_custom_call" | custom-call | tf_op jit(solution)/shard_map/em_step/pallas_call | solution.py:347
  56.6 13.1 %write_results.1 = (f32[1,128]{1,0:T(1,128)}, f32[32,3072]{1,0:T(8,128)}, f32[1,32]{1,0:T(1,128)}, f32[1,32]{1,0:T(1,128)}) custom-call(f32[1,128]{1,0:T(1,128)} %get-tuple-element.12.refs_0_, f32[32,3072]{1,0:T(8,128)} %get-tuple-element.13.refs_1_, f32[1,32]{1,0:T(1,128)} %get-tuple-element.14.refs_2_, f32[1,32]{1,0:T(1,128)} %get-tuple-element.15.refs_3_), custom_call_target="tpu_custom_call" | custom-call | tf_op jit(solution)/shard_map/write_results/pallas_call | solution.py:397

commit v3 on v2

--- a/solution.py
+++ b/solution.py
@@ -15,9 +15,9 @@
 
 def em_kernel(
     ncomp, npts, pieces,
-    points_ref, cand_ref, means_ref, shares_ref, var_ref, logw_ref,
-    loglik_ref, mean_ref, newvar_ref, newlogw_ref,
-    gathered, means, mu_old, cands, var_row, logw_row, aux, logp, stats, logliks, resp16, sums,
+    points_ref, cand_ref, means_ref, var_ref, logw_ref,
+    loglik_ref, wsum_ref, sums_ref,
+    gathered, means, cands, var_row, logw_row, aux, logp, stats, logliks, resp16, sums,
     wsend, land0, kept, relay1, land1, total, relay2, land2,
     load_sem, y_send, y_recv, sib_send, sib_recv, fwd_send, fwd_recv,
     aux_send, aux_recv, st_send, st_recv, sum_send, sum_recv,
@@ -35,10 +35,11 @@
     other_core = 1 - core
     sibling = y * 2 + other_core
     group = here_p // 4
-    stride0, stride1 = 1 + core, 2 - core
-    bit0, bit1 = (here_p // stride0) % 2, (here_p // stride1) % 2
-    partner0 = here_p + (1 - 2 * bit0) * stride0
-    partner1 = here_p + (1 - 2 * bit1) * stride1
+    bits = (here_p % 2, (here_p // 2) % 2)
+    partners = (here_p + 1 - 2 * bits[0], here_p + 2 - 4 * bits[1])
+
+    def order(c):
+        return (1, 0) if c % 4 == 1 else (0, 1)
 
     barrier = pltpu.get_barrier_semaphore()
     for k in range(1, ncomp):
@@ -53,26 +54,27 @@
     loads = [
         pltpu.make_async_copy(src, dst, load_sem.at[i])
         for i, (src, dst) in enumerate(
-            [
-                (points_ref, gathered.at[here_c]), (cand_ref, cands), (means_ref, means),
-                (var_ref, var_row), (logw_ref, logw_row), (shares_ref.at[here_p], mu_old),
+            [(cand_ref, cands)]
+            + [
+                (points_ref.at[:, pl.ds(c * piece, piece)], gathered.at[here_c, c])
+                for c in range(pieces)
             ]
+            + [(means_ref, means), (var_ref, var_row), (logw_ref, logw_row)]
         )
     ]
     for load in loads:
         load.start()
 
-    def add_square(ref):
-        def body(j, acc):
-            x = ref[:, pl.ds(pl.multiple_of(j * LANES, LANES), LANES)].astype(jnp.float32)
-            return acc + x * x
-        return body
-
-    loads[0].wait()
-    loads[1].wait()
-    sq = lax.fori_loop(
-        0, width // LANES, add_square(gathered.at[here_c]), jnp.zeros((rows, LANES), jnp.float32)
-    )
+    for load in loads[: pieces + 1]:
+        load.wait()
+
+    def add_point_squares(c, acc):
+        for j in range(piece // LANES):
+            x = gathered[here_c, c, :, j * LANES : (j + 1) * LANES].astype(jnp.float32)
+            acc = acc + x * x
+        return acc
+
+    sq = lax.fori_loop(0, pieces, add_point_squares, jnp.zeros((rows, LANES), jnp.float32))
     xx_row = jnp.sum(sq.T, axis=0, keepdims=True)
     aux[here_c] = jnp.concatenate(
         [cands[...].astype(jnp.float32), xx_row]
@@ -98,7 +100,7 @@
         ).wait_recv()
 
     def part(slot, c):
-        return gathered.at[slot, :, pl.ds(c * piece, piece)]
+        return gathered.at[slot, c]
 
     for c in range(pieces):
         for k in range(1, ny):
@@ -111,17 +113,27 @@
     send(gathered.at[here_c], gathered.at[here_c], sib_send.at[0], sib_recv.at[0],
          (here_p, sibling))
 
-    for load in loads[2:]:
+    for load in loads[pieces + 1 :]:
         load.wait()
 
-    def dot_t(slot, lo, size):
+    def dot_t(slot, c):
         return lax.dot_general(
-            means[:, pl.ds(lo, size)], gathered[slot, :, pl.ds(lo, size)],
+            means[:, pl.ds(c * piece, piece)], gathered[slot, c],
             (((1,), (1,)), ((), ())), preferred_element_type=jnp.float32,
         )
 
+    def dot_all(slot):
+        g = dot_t(slot, 0)
+        for c in range(1, pieces):
+            g = g + dot_t(slot, c)
+        return g
+
+    def add_mean_squares(j, acc):
+        x = means[:, pl.ds(pl.multiple_of(j * LANES, LANES), LANES)].astype(jnp.float32)
+        return acc + x * x
+
     sq = lax.fori_loop(
-        0, width // LANES, add_square(means), jnp.zeros((owned, LANES), jnp.float32)
+        0, width // LANES, add_mean_squares, jnp.zeros((owned, LANES), jnp.float32)
     )
     mm = jnp.sum(sq, axis=1, keepdims=True)
     eye_k = lax.broadcasted_iota(jnp.int32, (owned, owned), 0) == lax.broadcasted_iota(
@@ -160,14 +172,14 @@
             send(stats.at[here_c, s], stats.at[here_c, s], st_send.at[k - 1, s],
                  st_recv.at[k - 1, s], (here_p, (here_c + k) % ncomp))
 
-    finish(here_c, dot_t(here_c, 0, width))
+    finish(here_c, dot_all(here_c))
     for k in range(1, ncomp):
         arrived(aux.at[(here_c + ncomp - k) % ncomp], aux_send.at[k - 1], aux_recv.at[k - 1])
     arrived(gathered.at[sibling], sib_send.at[0], sib_recv.at[0])
-    finish(sibling, dot_t(sibling, 0, width))
+    finish(sibling, dot_all(sibling))
 
     def accumulate(slot, c):
-        g = dot_t(slot, c * piece, piece)
+        g = dot_t(slot, c)
         if c:
             g = logp[slot] + g
         if c < pieces - 1:
@@ -218,42 +230,40 @@
             sq_sum[b] = sq_sum[b] + resp * xx
 
     def make(c):
-        cols = pl.ds(c * piece, piece)
-        data = gathered[:, :, cols].reshape(ncomp * rows, piece)
+        data = gathered[:, c].reshape(ncomp * rows, piece)
         w = jnp.dot(resp16[...], data, preferred_element_type=jnp.float32)
+        first, second = order(c)
         for g in range(ngroups):
-            for hi in range(2):
-                for lo in range(2):
-                    first = (g * 4 + hi * 2 + lo) * share
-                    wsend[lo + core * (hi - lo), hi + core * (lo - hi), g, :, cols] = w[
-                        first : first + share
-                    ].astype(jnp.bfloat16)
-        send(wsend.at[1 - bit0, :, :, :, cols], land0.at[:, :, :, cols],
-             send0.at[c], recv0.at[c], (partner0, here_c))
+            for n in range(4):
+                dest = (n % 2, n // 2)
+                start = (g * 4 + n) * share
+                wsend[c, dest[first], dest[second], g] = w[start : start + share].astype(
+                    jnp.bfloat16
+                )
+        send(wsend.at[c, 1 - bits[first]], land0.at[c], send0.at[c], recv0.at[c],
+             (partners[first], here_c))
 
     def halve(c):
-        cols = pl.ds(c * piece, piece)
-        arrived(land0.at[:, :, :, cols], send0.at[c], recv0.at[c])
-        relay1[:, :, cols] = (
-            wsend[bit0, 1 - bit1, :, :, cols].astype(jnp.float32)
-            + land0[1 - bit1, :, :, cols].astype(jnp.float32)
+        first, second = order(c)
+        mine, other = bits[second], 1 - bits[second]
+        arrived(land0.at[c], send0.at[c], recv0.at[c])
+        relay1[c] = (
+            wsend[c, bits[first], other].astype(jnp.float32) + land0[c, other].astype(jnp.float32)
         ).astype(jnp.bfloat16)
-        send(relay1.at[:, :, cols], land1.at[:, :, cols], send1.at[c], recv1.at[c],
-             (partner1, here_c))
-        kept[:, :, cols] = wsend[bit0, bit1, :, :, cols].astype(jnp.float32) + land0[
-            bit1, :, :, cols
-        ].astype(jnp.float32)
+        send(relay1.at[c], land1.at[c], send1.at[c], recv1.at[c], (partners[second], here_c))
+        kept[c] = wsend[c, bits[first], mine].astype(jnp.float32) + land0[c, mine].astype(
+            jnp.float32
+        )
 
     def spread(c):
-        cols = pl.ds(c * piece, piece)
-        arrived(land1.at[:, :, cols], send1.at[c], recv1.at[c])
-        both = kept[:, :, cols] + land1[:, :, cols].astype(jnp.float32)
-        relay2[:, :, cols] = both.astype(jnp.bfloat16)
+        arrived(land1.at[c], send1.at[c], recv1.at[c])
+        both = kept[c] + land1[c].astype(jnp.float32)
+        relay2[c] = both.astype(jnp.bfloat16)
         for k in range(1, ngroups):
             to = (group + k) % ngroups
-            send(relay2.at[to, :, cols], land2.at[k - 1, :, cols],
-                 send2.at[k - 1, c], recv2.at[k - 1, c], (to * 4 + here_p % 4, here_c))
-        total[:, :, cols] = both
+            send(relay2.at[c, to], land2.at[k - 1, c], send2.at[k - 1, c], recv2.at[k - 1, c],
+                 (to * 4 + here_p % 4, here_c))
+        total[c] = both
 
     def share_sums():
         loglik_ref[...] = logliks[here_c]
@@ -265,19 +275,13 @@
             send(sums.at[0], sums.at[k], sum_send.at[k - 1], sum_recv.at[k - 1],
                  ((here_p + k) % npts, here_c))
 
-    def column(row):
-        mine = lax.broadcasted_iota(jnp.int32, (share, owned), 1) == (
-            lax.broadcasted_iota(jnp.int32, (share, owned), 0) + here_p * share
-        )
-        return jnp.sum(jnp.where(mine, row, 0.0), axis=1, keepdims=True)
-
     def take_sums():
         for k in range(1, npts):
             arrived(sums.at[k], sum_send.at[k - 1], sum_recv.at[k - 1])
         both = sums[0]
         for k in range(1, npts):
             both = both + sums[k]
-        return column(both[0:1]), column(both[1:2])
+        sums_ref[...] = both
 
     lag = 2
     for t in range(pieces + lag + 2):
@@ -290,45 +294,62 @@
         if lag < t <= pieces + lag:
             spread(t - lag - 1)
         if t == pieces:
-            counts, sqsum = take_sums()
-            scale = 1.0 / (counts + 1.0)
-            var_old = column(var_row[...])
-            cross = jnp.zeros((share, 1), jnp.float32)
-            norm = jnp.zeros((share, 1), jnp.float32)
+            take_sums()
         if t >= pieces:
             ready = [t - lag - 2] if t > pieces else list(range(pieces - lag - 1))
             for c in ready:
-                cols = pl.ds(c * piece, piece)
-                w = total[group, :, cols]
+                w = total[c, group]
                 for k in range(1, ngroups):
-                    arrived(land2.at[k - 1, :, cols], send2.at[k - 1, c], recv2.at[k - 1, c])
-                    w = w + land2[k - 1, :, cols].astype(jnp.float32)
-                new = (w + mu_old[:, cols].astype(jnp.float32)) * scale
-                mean_ref[:, cols] = new
-                cross = cross + jnp.sum(new * w, axis=1, keepdims=True)
-                norm = norm + jnp.sum(new * new, axis=1, keepdims=True)
+                    arrived(land2.at[k - 1, c], send2.at[k - 1, c], recv2.at[k - 1, c])
+                    w = w + land2[k - 1, c].astype(jnp.float32)
+                wsum_ref[:, c * piece : (c + 1) * piece] = w
+
+    for copy in sends:
+        copy.wait_send()
+
+
+def update_kernel(
+    npoints, ncomponents,
+    loglik_ref, wsum_ref, sums_ref, shares_ref, var_ref,
+    loglik_out, mean_ref, newvar_ref, newlogw_ref,
+    mu_old, load_sem,
+):
+    here_p = lax.axis_index("pts")
+    load = pltpu.make_async_copy(shares_ref.at[here_p], mu_old, load_sem)
+    load.start()
+    share, width = wsum_ref.shape
+    owned = sums_ref.shape[1]
+    mine = lax.broadcasted_iota(jnp.int32, (share, owned), 1) == (
+        lax.broadcasted_iota(jnp.int32, (share, owned), 0) + here_p * share
+    )
+
+    def column(row):
+        return jnp.sum(jnp.where(mine, row, 0.0), axis=1, keepdims=True)
+
+    loglik_out[...] = loglik_ref[...]
+    counts, sqsum = column(sums_ref[0:1, :]), column(sums_ref[1:2, :])
+    var_old = column(var_ref[...])
+    scale = 1.0 / (counts + 1.0)
+    cross = jnp.zeros((share, LANES), jnp.float32)
+    norm = jnp.zeros((share, LANES), jnp.float32)
+    load.wait()
+    for j in range(width // LANES):
+        cols = slice(j * LANES, (j + 1) * LANES)
+        w = wsum_ref[:, cols]
+        new = (w + mu_old[:, cols].astype(jnp.float32)) * scale
+        mean_ref[:, cols] = new
+        cross = cross + new * w
+        norm = norm + new * new
+    cross = jnp.sum(cross, axis=1, keepdims=True)
+    norm = jnp.sum(norm, axis=1, keepdims=True)
     resid = sqsum - 2.0 * cross + counts * norm + width * var_old
     new_var = resid / (width * (counts + 1.0))
-    new_logw = jnp.log((counts + 1.0) / float(rows * ncomp * npts + owned * ncomp))
-    eye_s = lax.broadcasted_iota(jnp.int32, (share, share), 0) == lax.broadcasted_iota(
+    new_logw = jnp.log((counts + 1.0) / float(npoints + ncomponents))
+    eye = lax.broadcasted_iota(jnp.int32, (share, share), 0) == lax.broadcasted_iota(
         jnp.int32, (share, share), 1
     )
-    newvar_ref[...] = jnp.sum(jnp.where(eye_s, new_var, 0.0), axis=0, keepdims=True)
-    newlogw_ref[...] = jnp.sum(jnp.where(eye_s, new_logw, 0.0), axis=0, keepdims=True)
-
-    for copy in sends:
-        copy.wait_send()
-
-
-def copy_kernel(*refs):
-    count = len(refs) // 2
-    copies = [
-        pltpu.make_async_copy(refs[i], refs[count + i], refs[-1].at[i]) for i in range(count)
-    ]
-    for copy in copies:
-        copy.start()
-    for copy in copies:
-        copy.wait()
+    newvar_ref[...] = jnp.sum(jnp.where(eye, new_var, 0.0), axis=0, keepdims=True)
+    newlogw_ref[...] = jnp.sum(jnp.where(eye, new_logw, 0.0), axis=0, keepdims=True)
 
 
 def on_device(ncomp, npts, points, candidates, means, variances, log_weights):
@@ -344,20 +365,19 @@
     dma = pltpu.SemaphoreType.DMA
     vmem = pl.BlockSpec(memory_space=pltpu.VMEM)
     anywhere = pl.BlockSpec(memory_space=pl.ANY)
-    results = pl.pallas_call(
+    piece = width // pieces
+    loglik, wsum, sums = pl.pallas_call(
         functools.partial(em_kernel, ncomp, npts, pieces),
         out_shape=(
             jax.ShapeDtypeStruct((1, rows), f32),
             jax.ShapeDtypeStruct((share, width), f32),
-            jax.ShapeDtypeStruct((1, share), f32),
-            jax.ShapeDtypeStruct((1, share), f32),
+            jax.ShapeDtypeStruct((2, owned), f32),
         ),
-        in_specs=[anywhere] * 6,
-        out_specs=(vmem, vmem, vmem, vmem),
+        in_specs=[anywhere] * 5,
+        out_specs=(vmem, vmem, vmem),
         scratch_shapes=[
-            pltpu.VMEM((ncomp, rows, width), bf16),
+            pltpu.VMEM((ncomp, pieces, rows, piece), bf16),
             pltpu.VMEM((owned, width), bf16),
-            pltpu.VMEM((share, width), bf16),
             pltpu.VMEM((ncand, rows), jnp.int32),
             pltpu.VMEM((1, owned), f32),
             pltpu.VMEM((1, owned), f32),
@@ -367,15 +387,15 @@
             pltpu.VMEM((ncomp, 1, rows), f32),
             pltpu.VMEM((owned, ncomp * rows), bf16),
             pltpu.VMEM((npts, 2, owned), f32),
-            pltpu.VMEM((2, 2, ngroups, share, width), bf16),
-            pltpu.VMEM((2, ngroups, share, width), bf16),
-            pltpu.VMEM((ngroups, share, width), f32),
-            pltpu.VMEM((ngroups, share, width), bf16),
-            pltpu.VMEM((ngroups, share, width), bf16),
-            pltpu.VMEM((ngroups, share, width), f32),
-            pltpu.VMEM((ngroups, share, width), bf16),
-            pltpu.VMEM((ngroups - 1, share, width), bf16),
-            dma((6,)),
+            pltpu.VMEM((pieces, 2, 2, ngroups, share, piece), bf16),
+            pltpu.VMEM((pieces, 2, ngroups, share, piece), bf16),
+            pltpu.VMEM((pieces, ngroups, share, piece), f32),
+            pltpu.VMEM((pieces, ngroups, share, piece), bf16),
+            pltpu.VMEM((pieces, ngroups, share, piece), bf16),
+            pltpu.VMEM((pieces, ngroups, share, piece), f32),
+            pltpu.VMEM((pieces, ngroups, share, piece), bf16),
+            pltpu.VMEM((ngroups - 1, pieces, share, piece), bf16),
+            dma((pieces + 4,)),
             dma((ny - 1, pieces)), dma((ny - 1, pieces)),
             dma((1,)), dma((1,)),
             dma((ny - 1, pieces)), dma((ny - 1, pieces)),
@@ -391,18 +411,22 @@
         ),
         name="em_step",
     )(
-        points, candidates.T, means, means.reshape(npts, share, width),
-        variances.reshape(1, owned), log_weights.reshape(1, owned),
+        points, candidates.T, means, variances.reshape(1, owned), log_weights.reshape(1, owned)
     )
     loglik, new_means, new_var, new_logw = pl.pallas_call(
-        copy_kernel,
-        out_shape=tuple(jax.ShapeDtypeStruct(x.shape, x.dtype) for x in results),
-        in_specs=[anywhere] * len(results),
-        out_specs=(anywhere,) * len(results),
-        scratch_shapes=[dma((len(results),))],
+        functools.partial(update_kernel, rows * ncomp * npts, owned * ncomp),
+        out_shape=(
+            jax.ShapeDtypeStruct((1, rows), f32),
+            jax.ShapeDtypeStruct((share, width), f32),
+            jax.ShapeDtypeStruct((1, share), f32),
+            jax.ShapeDtypeStruct((1, share), f32),
+        ),
+        in_specs=[vmem, vmem, vmem, anywhere, vmem],
+        out_specs=(vmem, vmem, vmem, vmem),
+        scratch_shapes=[pltpu.VMEM((share, width), bf16), dma],
         compiler_params=pltpu.CompilerParams(vmem_limit_bytes=60 * 1024 * 1024),
-        name="write_results",
-    )(*results)
+        name="update",
+    )(loglik, wsum, sums, means.reshape(npts, share, width), variances.reshape(1, owned))
     return (
         loglik.reshape(rows),
         new_means.reshape(1, share, width),

time: 69.8 us -> 61.8 us (0.89)
  Pallas kernels: 69 us -> 60.9 us
    pallas_call x1, Pallas kernels: 13.1 us -> 2.76 us  [on_device(): pl.pallas_call(functools.partial(update_kernel, rows * ncomp * npts, owne...]
    pallas_call x1, Pallas kernels: 55.9 us -> 58.2 us  [on_device(): pl.pallas_call(functools.partial(em_kernel, ncomp, npts, pieces), out_sha...]
where the time goes in v3:
time: 61.8 us; the launch traced here: 61.6 us
  Pallas kernels  60.9 us (99%)
  between operations  0.64 us (1%)
    pallas_call x1, Pallas kernels, on_device(): pl.pallas_call(functools.partial(em_kernel, ncomp, npts, pieces), out_sha...  58.2 us
    pallas_call x1, Pallas kernels, on_device(): pl.pallas_call(functools.partial(update_kernel, rows * ncomp * npts, owne...  2.76 us

profile of v3, /device:TPU:0, one launch (start us, length us, event | category | flops | bytes accessed | tf_op | source)
XLA Modules:
  0.0 61.6 jit_solution(17128354339936598199)
XLA Ops:
  0.6 58.2 %em_step.1 = (f32[1,128]{1,0:T(1,128)}, f32[32,3072]{1,0:T(8,128)}, f32[2,256]{1,0:T(2,128)}) custom-call(bf16[128,3072]{1,0:T(8,128)(2,1)} %points_ref.1, s32[4,128]{1,0:T(4,128)} %bitcast.9, bf16[256,3072]{1,0:T(8,128)(2,1)} %means_ref.1, f32[1,256]{1,0:T(1,128)} %bitcast.7, f32[1,256]{1,0:T(1,128)} %bitcast.10), custom_call_target="tpu_custom_call" | custom-call | tf_op jit(solution)/shard_map/em_step/pallas_call | solution.py:369
  58.8 2.8 %update.1 = (f32[1,128]{1,0:T(1,128)}, f32[32,3072]{1,0:T(8,128)}, f32[1,32]{1,0:T(1,128)}, f32[1,32]{1,0:T(1,128)}) custom-call(f32[1,128]{1,0:T(1,128)} %get-tuple-element.11.loglik_ref, f32[32,3072]{1,0:T(8,128)} %get-tuple-element.12.wsum_ref, f32[2,256]{1,0:T(2,128)} %get-tuple-element.13.sums_ref, bf16[8,32,3072]{2,1,0:T(8,128)(2,1)} %bitcast.6, ...), custom_call_target="tpu_custom_call" | custom-call | tf_op jit(solution)/shard_map/update/pallas_call | solution.py:416

commit v4 on v3

--- a/solution.py
+++ b/solution.py
@@ -283,26 +283,23 @@
             both = both + sums[k]
         sums_ref[...] = both
 
-    lag = 2
-    for t in range(pieces + lag + 2):
+    for c in range(pieces):
+        make(c)
+    share_sums()
+    for t in range(pieces + 2):
         if t < pieces:
-            make(t)
-        if t == 1:
-            share_sums()
-        if lag <= t < pieces + lag:
-            halve(t - lag)
-        if lag < t <= pieces + lag:
-            spread(t - lag - 1)
-        if t == pieces:
+            halve(t)
+        if 1 <= t <= pieces:
+            spread(t - 1)
+        if t == 2:
             take_sums()
-        if t >= pieces:
-            ready = [t - lag - 2] if t > pieces else list(range(pieces - lag - 1))
-            for c in ready:
-                w = total[c, group]
-                for k in range(1, ngroups):
-                    arrived(land2.at[k - 1, c], send2.at[k - 1, c], recv2.at[k - 1, c])
-                    w = w + land2[k - 1, c].astype(jnp.float32)
-                wsum_ref[:, c * piece : (c + 1) * piece] = w
+        if t >= 2:
+            c = t - 2
+            w = total[c, group]
+            for k in range(1, ngroups):
+                arrived(land2.at[k - 1, c], send2.at[k - 1, c], recv2.at[k - 1, c])
+                w = w + land2[k - 1, c].astype(jnp.float32)
+            wsum_ref[:, c * piece : (c + 1) * piece] = w
 
     for copy in sends:
         copy.wait_send()

time: 61.8 us -> 65.6 us (1.061)
  Pallas kernels: 60.9 us -> 64.8 us
    pallas_call x1, Pallas kernels: 58.2 us -> 62 us  [on_device(): pl.pallas_call(functools.partial(em_kernel, ncomp, npts, pieces), out_sha...]
where the time goes in v4:
time: 65.6 us; the launch traced here: 65.4 us
  Pallas kernels  64.8 us (99%)
    pallas_call x1, Pallas kernels, on_device(): pl.pallas_call(functools.partial(em_kernel, ncomp, npts, pieces), out_sha...  62 us
    pallas_call x1, Pallas kernels, on_device(): pl.pallas_call(functools.partial(update_kernel, rows * ncomp * npts, owne...  2.76 us

profile of v4, /device:TPU:0, one launch (start us, length us, event | category | flops | bytes accessed | tf_op | source)
XLA Modules:
  0.0 65.4 jit_solution(14432907758265184891)
XLA Ops:
  0.6 62.0 %em_step.1 = (f32[1,128]{1,0:T(1,128)}, f32[32,3072]{1,0:T(8,128)}, f32[2,256]{1,0:T(2,128)}) custom-call(bf16[128,3072]{1,0:T(8,128)(2,1)} %points_ref.1, s32[4,128]{1,0:T(4,128)} %bitcast.9, bf16[256,3072]{1,0:T(8,128)(2,1)} %means_ref.1, f32[1,256]{1,0:T(1,128)} %bitcast.7, f32[1,256]{1,0:T(1,128)} %bitcast.10), custom_call_target="tpu_custom_call" | custom-call | tf_op jit(solution)/shard_map/em_step/pallas_call | solution.py:366
  62.7 2.8 %update.1 = (f32[1,128]{1,0:T(1,128)}, f32[32,3072]{1,0:T(8,128)}, f32[1,32]{1,0:T(1,128)}, f32[1,32]{1,0:T(1,128)}) custom-call(f32[1,128]{1,0:T(1,128)} %get-tuple-element.11.loglik_ref, f32[32,3072]{1,0:T(8,128)} %get-tuple-element.12.wsum_ref, f32[2,256]{1,0:T(2,128)} %get-tuple-element.13.sums_ref, bf16[8,32,3072]{2,1,0:T(8,128)(2,1)} %bitcast.6, ...), custom_call_target="tpu_custom_call" | custom-call | tf_op jit(solution)/shard_map/update/pallas_call | solution.py:413

commit v5 on v3

--- a/solution.py
+++ b/solution.py
@@ -17,7 +17,7 @@
     ncomp, npts, pieces,
     points_ref, cand_ref, means_ref, var_ref, logw_ref,
     loglik_ref, wsum_ref, sums_ref,
-    gathered, means, cands, var_row, logw_row, aux, logp, stats, logliks, resp16, sums,
+    gathered, means, cands, var_row, logw_row, aux, partial, logp, stats, logliks, resp16, sums,
     wsend, land0, kept, relay1, land1, total, relay2, land2,
     load_sem, y_send, y_recv, sib_send, sib_recv, fwd_send, fwd_recv,
     aux_send, aux_recv, st_send, st_recv, sum_send, sum_recv,
@@ -39,7 +39,7 @@
     partners = (here_p + 1 - 2 * bits[0], here_p + 2 - 4 * bits[1])
 
     def order(c):
-        return (1, 0) if c % 4 == 1 else (0, 1)
+        return (1, 0) if c == 1 else (0, 1)
 
     barrier = pltpu.get_barrier_semaphore()
     for k in range(1, ncomp):
@@ -56,7 +56,7 @@
         for i, (src, dst) in enumerate(
             [(cand_ref, cands)]
             + [
-                (points_ref.at[:, pl.ds(c * piece, piece)], gathered.at[here_c, c])
+                (points_ref.at[:, pl.ds(c * piece, piece)], gathered.at[c, here_c])
                 for c in range(pieces)
             ]
             + [(means_ref, means), (var_ref, var_row), (logw_ref, logw_row)]
@@ -70,7 +70,7 @@
 
     def add_point_squares(c, acc):
         for j in range(piece // LANES):
-            x = gathered[here_c, c, :, j * LANES : (j + 1) * LANES].astype(jnp.float32)
+            x = gathered[c, here_c, :, j * LANES : (j + 1) * LANES].astype(jnp.float32)
             acc = acc + x * x
         return acc
 
@@ -100,33 +100,26 @@
         ).wait_recv()
 
     def part(slot, c):
-        return gathered.at[slot, c]
+        return gathered.at[c, slot]
 
     for c in range(pieces):
         for k in range(1, ny):
             send(part(here_c, c), part(here_c, c), y_send.at[k - 1, c], y_recv.at[k - 1, c],
                  (here_p, ((y + k) % ny) * 2 + core))
+        send(part(here_c, c), part(here_c, c), sib_send.at[c], sib_recv.at[c], (here_p, sibling))
         if c == 0:
             for k in range(1, ncomp):
                 send(aux.at[here_c], aux.at[here_c], aux_send.at[k - 1], aux_recv.at[k - 1],
                      (here_p, (here_c + k) % ncomp))
-    send(gathered.at[here_c], gathered.at[here_c], sib_send.at[0], sib_recv.at[0],
-         (here_p, sibling))
-
     for load in loads[pieces + 1 :]:
         load.wait()
 
-    def dot_t(slot, c):
+    def pair_dot(chip, c):
+        rows2 = gathered[c, pl.ds(2 * chip, 2)].reshape(2 * rows, piece)
         return lax.dot_general(
-            means[:, pl.ds(c * piece, piece)], gathered[slot, c],
+            means[:, pl.ds(c * piece, piece)], rows2,
             (((1,), (1,)), ((), ())), preferred_element_type=jnp.float32,
         )
-
-    def dot_all(slot):
-        g = dot_t(slot, 0)
-        for c in range(1, pieces):
-            g = g + dot_t(slot, c)
-        return g
 
     def add_mean_squares(j, acc):
         x = means[:, pl.ds(pl.multiple_of(j * LANES, LANES), LANES)].astype(jnp.float32)
@@ -172,34 +165,38 @@
             send(stats.at[here_c, s], stats.at[here_c, s], st_send.at[k - 1, s],
                  st_recv.at[k - 1, s], (here_p, (here_c + k) % ncomp))
 
-    finish(here_c, dot_all(here_c))
-    for k in range(1, ncomp):
-        arrived(aux.at[(here_c + ncomp - k) % ncomp], aux_send.at[k - 1], aux_recv.at[k - 1])
-    arrived(gathered.at[sibling], sib_send.at[0], sib_recv.at[0])
-    finish(sibling, dot_all(sibling))
-
-    def accumulate(slot, c):
-        g = dot_t(slot, c)
+    def add_pair(chip, c):
+        g = pair_dot(chip, c)
         if c:
-            g = logp[slot] + g
+            g = partial[chip] + g
         if c < pieces - 1:
-            logp[slot] = g
+            partial[chip] = g
         else:
-            finish(slot, g)
+            for j in range(2):
+                finish(2 * chip + j, g[:, j * rows : (j + 1) * rows])
 
     def take_forwarded(c):
         for k in range(1, ny):
-            slot = ((y + ny - k) % ny) * 2 + other_core
-            arrived(part(slot, c), fwd_send.at[k - 1, c], fwd_recv.at[k - 1, c])
-            accumulate(slot, c)
-
+            chip = (y + ny - k) % ny
+            arrived(part(chip * 2 + other_core, c), fwd_send.at[k - 1, c], fwd_recv.at[k - 1, c])
+            add_pair(chip, c)
+
+    own = 0
     for c in range(pieces):
         for k in range(1, ny):
             slot = ((y + ny - k) % ny) * 2 + core
             arrived(part(slot, c), y_send.at[k - 1, c], y_recv.at[k - 1, c])
             send(part(slot, c), part(slot, c), fwd_send.at[k - 1, c], fwd_recv.at[k - 1, c],
                  (here_p, sibling))
-            accumulate(slot, c)
+        if c == 0:
+            for k in range(1, ncomp):
+                arrived(aux.at[(here_c + ncomp - k) % ncomp], aux_send.at[k - 1],
+                        aux_recv.at[k - 1])
+        for _ in range(2):
+            if own < pieces:
+                arrived(part(sibling, own), sib_send.at[own], sib_recv.at[own])
+                add_pair(y, own)
+                own += 1
         if c:
             take_forwarded(c - 1)
     take_forwarded(pieces - 1)
@@ -230,7 +227,7 @@
             sq_sum[b] = sq_sum[b] + resp * xx
 
     def make(c):
-        data = gathered[:, c].reshape(ncomp * rows, piece)
+        data = gathered[c].reshape(ncomp * rows, piece)
         w = jnp.dot(resp16[...], data, preferred_element_type=jnp.float32)
         first, second = order(c)
         for g in range(ngroups):
@@ -295,14 +292,13 @@
             spread(t - lag - 1)
         if t == pieces:
             take_sums()
-        if t >= pieces:
-            ready = [t - lag - 2] if t > pieces else list(range(pieces - lag - 1))
-            for c in ready:
-                w = total[c, group]
-                for k in range(1, ngroups):
-                    arrived(land2.at[k - 1, c], send2.at[k - 1, c], recv2.at[k - 1, c])
-                    w = w + land2[k - 1, c].astype(jnp.float32)
-                wsum_ref[:, c * piece : (c + 1) * piece] = w
+        if t >= lag + 2:
+            c = t - lag - 2
+            w = total[c, group]
+            for k in range(1, ngroups):
+                arrived(land2.at[k - 1, c], send2.at[k - 1, c], recv2.at[k - 1, c])
+                w = w + land2[k - 1, c].astype(jnp.float32)
+            wsum_ref[:, c * piece : (c + 1) * piece] = w
 
     for copy in sends:
         copy.wait_send()
@@ -357,7 +353,7 @@
     owned = means.shape[0]
     share = owned // npts
     ngroups = npts // 4
-    pieces = 8
+    pieces = 6
     ncand = candidates.shape[1]
     ny = ncomp // 2
     aux_rows = -(-(ncand + 1) // 8) * 8
@@ -376,12 +372,13 @@
         in_specs=[anywhere] * 5,
         out_specs=(vmem, vmem, vmem),
         scratch_shapes=[
-            pltpu.VMEM((ncomp, pieces, rows, piece), bf16),
+            pltpu.VMEM((pieces, ncomp, rows, piece), bf16),
             pltpu.VMEM((owned, width), bf16),
             pltpu.VMEM((ncand, rows), jnp.int32),
             pltpu.VMEM((1, owned), f32),
             pltpu.VMEM((1, owned), f32),
             pltpu.VMEM((ncomp, aux_rows, rows), f32),
+            pltpu.VMEM((ny, owned, 2 * rows), f32),
             pltpu.VMEM((ncomp, owned, rows), f32),
             pltpu.VMEM((ncomp, ncomp, 2, rows), f32),
             pltpu.VMEM((ncomp, 1, rows), f32),
@@ -397,7 +394,7 @@
             pltpu.VMEM((ngroups - 1, pieces, share, piece), bf16),
             dma((pieces + 4,)),
             dma((ny - 1, pieces)), dma((ny - 1, pieces)),
-            dma((1,)), dma((1,)),
+            dma((pieces,)), dma((pieces,)),
             dma((ny - 1, pieces)), dma((ny - 1, pieces)),
             dma((ncomp - 1,)), dma((ncomp - 1,)),
             dma((ncomp - 1, ncomp)), dma((ncomp - 1, ncomp)),

time: 61.8 us -> 58.5 us (0.947)
  Pallas kernels: 60.9 us -> 57.7 us
    pallas_call x1, Pallas kernels: 58.2 us -> 54.9 us  [on_device(): pl.pallas_call(functools.partial(em_kernel, ncomp, npts, pieces), out_sha...]
where the time goes in v5:
time: 58.5 us; the launch traced here: 58.3 us
  Pallas kernels  57.7 us (99%)
  between operations  0.64 us (1%)
    pallas_call x1, Pallas kernels, on_device(): pl.pallas_call(functools.partial(em_kernel, ncomp, npts, pieces), out_sha...  54.9 us
    pallas_call x1, Pallas kernels, on_device(): pl.pallas_call(functools.partial(update_kernel, rows * ncomp * npts, owne...  2.76 us

profile of v5, /device:TPU:0, one launch (start us, length us, event | category | flops | bytes accessed | tf_op | source)
XLA Modules:
  0.0 58.3 jit_solution(7975847048564022834)
XLA Ops:
  0.6 54.9 %em_step.1 = (f32[1,128]{1,0:T(1,128)}, f32[32,3072]{1,0:T(8,128)}, f32[2,256]{1,0:T(2,128)}) custom-call(bf16[128,3072]{1,0:T(8,128)(2,1)} %points_ref.1, s32[4,128]{1,0:T(4,128)} %bitcast.9, bf16[256,3072]{1,0:T(8,128)(2,1)} %means_ref.1, f32[1,256]{1,0:T(1,128)} %bitcast.7, f32[1,256]{1,0:T(1,128)} %bitcast.10), custom_call_target="tpu_custom_call" | custom-call | tf_op jit(solution)/shard_map/em_step/pallas_call | solution.py:365
  55.6 2.8 %update.1 = (f32[1,128]{1,0:T(1,128)}, f32[32,3072]{1,0:T(8,128)}, f32[1,32]{1,0:T(1,128)}, f32[1,32]{1,0:T(1,128)}) custom-call(f32[1,128]{1,0:T(1,128)} %get-tuple-element.11.loglik_ref, f32[32,3072]{1,0:T(8,128)} %get-tuple-element.12.wsum_ref, f32[2,256]{1,0:T(2,128)} %get-tuple-element.13.sums_ref, bf16[8,32,3072]{2,1,0:T(8,128)(2,1)} %bitcast.6, ...), custom_call_target="tpu_custom_call" | custom-call | tf_op jit(solution)/shard_map/update/pallas_call | solution.py:413

commit v6 on v5

--- a/solution.py
+++ b/solution.py
@@ -35,11 +35,10 @@
     other_core = 1 - core
     sibling = y * 2 + other_core
     group = here_p // 4
-    bits = (here_p % 2, (here_p // 2) % 2)
-    partners = (here_p + 1 - 2 * bits[0], here_p + 2 - 4 * bits[1])
-
-    def order(c):
-        return (1, 0) if c == 1 else (0, 1)
+    bit0, bit1 = here_p % 2, (here_p // 2) % 2
+    bits = (bit0 + core * (bit1 - bit0), bit1 + core * (bit0 - bit1))
+    strides = (1 + core, 2 - core)
+    partners = tuple(here_p + (1 - 2 * bit) * stride for bit, stride in zip(bits, strides))
 
     barrier = pltpu.get_barrier_semaphore()
     for k in range(1, ncomp):
@@ -102,15 +101,23 @@
     def part(slot, c):
         return gathered.at[c, slot]
 
-    for c in range(pieces):
+    def send_y(c):
         for k in range(1, ny):
             send(part(here_c, c), part(here_c, c), y_send.at[k - 1, c], y_recv.at[k - 1, c],
                  (here_p, ((y + k) % ny) * 2 + core))
+
+    def send_sibling(c):
         send(part(here_c, c), part(here_c, c), sib_send.at[c], sib_recv.at[c], (here_p, sibling))
+
+    ahead = 2
+    for c in range(ahead):
+        send_y(c)
+        send_sibling(c)
         if c == 0:
             for k in range(1, ncomp):
                 send(aux.at[here_c], aux.at[here_c], aux_send.at[k - 1], aux_recv.at[k - 1],
                      (here_p, (here_c + k) % ncomp))
+
     for load in loads[pieces + 1 :]:
         load.wait()
 
@@ -188,6 +195,10 @@
             arrived(part(slot, c), y_send.at[k - 1, c], y_recv.at[k - 1, c])
             send(part(slot, c), part(slot, c), fwd_send.at[k - 1, c], fwd_recv.at[k - 1, c],
                  (here_p, sibling))
+        if c + ahead < pieces:
+            send_y(c + ahead)
+        for n in range(ahead + 2 * c, min(pieces, ahead + 2 * c + 2)):
+            send_sibling(n)
         if c == 0:
             for k in range(1, ncomp):
                 arrived(aux.at[(here_c + ncomp - k) % ncomp], aux_send.at[k - 1],
@@ -229,26 +240,24 @@
     def make(c):
         data = gathered[c].reshape(ncomp * rows, piece)
         w = jnp.dot(resp16[...], data, preferred_element_type=jnp.float32)
-        first, second = order(c)
         for g in range(ngroups):
             for n in range(4):
-                dest = (n % 2, n // 2)
+                lo, hi = n % 2, n // 2
                 start = (g * 4 + n) * share
-                wsend[c, dest[first], dest[second], g] = w[start : start + share].astype(
-                    jnp.bfloat16
-                )
-        send(wsend.at[c, 1 - bits[first]], land0.at[c], send0.at[c], recv0.at[c],
-             (partners[first], here_c))
+                wsend[c, lo + core * (hi - lo), hi + core * (lo - hi), g] = w[
+                    start : start + share
+                ].astype(jnp.bfloat16)
+        send(wsend.at[c, 1 - bits[0]], land0.at[c], send0.at[c], recv0.at[c],
+             (partners[0], here_c))
 
     def halve(c):
-        first, second = order(c)
-        mine, other = bits[second], 1 - bits[second]
+        mine, other = bits[1], 1 - bits[1]
         arrived(land0.at[c], send0.at[c], recv0.at[c])
         relay1[c] = (
-            wsend[c, bits[first], other].astype(jnp.float32) + land0[c, other].astype(jnp.float32)
+            wsend[c, bits[0], other].astype(jnp.float32) + land0[c, other].astype(jnp.float32)
         ).astype(jnp.bfloat16)
-        send(relay1.at[c], land1.at[c], send1.at[c], recv1.at[c], (partners[second], here_c))
-        kept[c] = wsend[c, bits[first], mine].astype(jnp.float32) + land0[c, mine].astype(
+        send(relay1.at[c], land1.at[c], send1.at[c], recv1.at[c], (partners[1], here_c))
+        kept[c] = wsend[c, bits[0], mine].astype(jnp.float32) + land0[c, mine].astype(
             jnp.float32
         )
 

time: 58.5 us -> 57.6 us (0.985)
  Pallas kernels: 57.7 us -> 56.7 us
    pallas_call x1, Pallas kernels: 54.9 us -> 54 us  [on_device(): pl.pallas_call(functools.partial(em_kernel, ncomp, npts, pieces), out_sha...]
where the time goes in v6:
time: 57.6 us; the launch traced here: 57.4 us
  Pallas kernels  56.7 us (98%)
  between operations  0.64 us (1%)
    pallas_call x1, Pallas kernels, on_device(): pl.pallas_call(functools.partial(em_kernel, ncomp, npts, pieces), out_sha...  54 us
    pallas_call x1, Pallas kernels, on_device(): pl.pallas_call(functools.partial(update_kernel, rows * ncomp * npts, owne...  2.76 us

profile of v6, /device:TPU:0, one launch (start us, length us, event | category | flops | bytes accessed | tf_op | source)
XLA Modules:
  0.0 57.4 jit_solution(14989064118200025768)
XLA Ops:
  0.6 54.0 %em_step.1 = (f32[1,128]{1,0:T(1,128)}, f32[32,3072]{1,0:T(8,128)}, f32[2,256]{1,0:T(2,128)}) custom-call(bf16[128,3072]{1,0:T(8,128)(2,1)} %points_ref.1, s32[4,128]{1,0:T(4,128)} %bitcast.9, bf16[256,3072]{1,0:T(8,128)(2,1)} %means_ref.1, f32[1,256]{1,0:T(1,128)} %bitcast.7, f32[1,256]{1,0:T(1,128)} %bitcast.10), custom_call_target="tpu_custom_call" | custom-call | tf_op jit(solution)/shard_map/em_step/pallas_call | solution.py:374
  54.6 2.8 %update.1 = (f32[1,128]{1,0:T(1,128)}, f32[32,3072]{1,0:T(8,128)}, f32[1,32]{1,0:T(1,128)}, f32[1,32]{1,0:T(1,128)}) custom-call(f32[1,128]{1,0:T(1,128)} %get-tuple-element.11.loglik_ref, f32[32,3072]{1,0:T(8,128)} %get-tuple-element.12.wsum_ref, f32[2,256]{1,0:T(2,128)} %get-tuple-element.13.sums_ref, bf16[8,32,3072]{2,1,0:T(8,128)(2,1)} %bitcast.6, ...), custom_call_target="tpu_custom_call" | custom-call | tf_op jit(solution)/shard_map/update/pallas_call | solution.py:422

commit v7 on v6

--- a/solution.py
+++ b/solution.py
@@ -18,10 +18,10 @@
     points_ref, cand_ref, means_ref, var_ref, logw_ref,
     loglik_ref, wsum_ref, sums_ref,
     gathered, means, cands, var_row, logw_row, aux, partial, logp, stats, logliks, resp16, sums,
-    wsend, land0, kept, relay1, land1, total, relay2, land2,
+    wsend, land0, kept, relay1, land1, total, relay2, land2, wsum, both_sums,
     load_sem, y_send, y_recv, sib_send, sib_recv, fwd_send, fwd_recv,
     aux_send, aux_recv, st_send, st_recv, sum_send, sum_recv,
-    send0, recv0, send1, recv1, send2, recv2,
+    send0, recv0, send1, recv1, send2, recv2, out_sem,
 ):
     here_c, here_p = lax.axis_index("comp"), lax.axis_index("pts")
     ny, ngroups = ncomp // 2, npts // 4
@@ -82,7 +82,12 @@
     )
     pl.semaphore_wait(barrier, ncomp + npts - 2)
 
-    sends = []
+    sends, stores = [], []
+
+    def store(src, dst, i):
+        copy = pltpu.make_async_copy(src, dst, out_sem.at[i])
+        copy.start()
+        stores.append(copy)
 
     def send(src, dst, s_sem, r_sem, device):
         copy = pltpu.make_async_remote_copy(
@@ -272,7 +277,7 @@
         total[c] = both
 
     def share_sums():
-        loglik_ref[...] = logliks[here_c]
+        store(logliks.at[here_c], loglik_ref, 0)
         for b in range(2):
             cols = slice(b * block, (b + 1) * block)
             sums[0, 0:1, cols] = jnp.sum(count_sum[b].T, axis=0, keepdims=True)
@@ -287,7 +292,8 @@
         both = sums[0]
         for k in range(1, npts):
             both = both + sums[k]
-        sums_ref[...] = both
+        both_sums[...] = both
+        store(both_sums, sums_ref, 1)
 
     lag = 2
     for t in range(pieces + lag + 2):
@@ -307,21 +313,32 @@
             for k in range(1, ngroups):
                 arrived(land2.at[k - 1, c], send2.at[k - 1, c], recv2.at[k - 1, c])
                 w = w + land2[k - 1, c].astype(jnp.float32)
-            wsum_ref[:, c * piece : (c + 1) * piece] = w
-
+            wsum[c] = w
+            store(wsum.at[c], wsum_ref.at[:, pl.ds(c * piece, piece)], 2 + c)
+
+    for copy in stores:
+        copy.wait()
     for copy in sends:
         copy.wait_send()
 
 
 def update_kernel(
     npoints, ncomponents,
-    loglik_ref, wsum_ref, sums_ref, shares_ref, var_ref,
-    loglik_out, mean_ref, newvar_ref, newlogw_ref,
-    mu_old, load_sem,
+    loglik_in, wsum_in, sums_in, shares_ref, var_in,
+    loglik_out, mean_out, newvar_out, newlogw_out,
+    loglik, wsum_ref, sums_ref, mu_old, var_ref, mean_ref, newvar_ref, newlogw_ref,
+    load_sem, out_sem,
 ):
     here_p = lax.axis_index("pts")
-    load = pltpu.make_async_copy(shares_ref.at[here_p], mu_old, load_sem)
-    load.start()
+    pairs = [
+        (sums_in, sums_ref), (var_in, var_ref), (wsum_in, wsum_ref),
+        (shares_ref.at[here_p], mu_old), (loglik_in, loglik),
+    ]
+    loads = [
+        pltpu.make_async_copy(src, dst, load_sem.at[i]) for i, (src, dst) in enumerate(pairs)
+    ]
+    for load in loads:
+        load.start()
     share, width = wsum_ref.shape
     owned = sums_ref.shape[1]
     mine = lax.broadcasted_iota(jnp.int32, (share, owned), 1) == (
@@ -331,13 +348,13 @@
     def column(row):
         return jnp.sum(jnp.where(mine, row, 0.0), axis=1, keepdims=True)
 
-    loglik_out[...] = loglik_ref[...]
+    for load in loads:
+        load.wait()
     counts, sqsum = column(sums_ref[0:1, :]), column(sums_ref[1:2, :])
     var_old = column(var_ref[...])
     scale = 1.0 / (counts + 1.0)
     cross = jnp.zeros((share, LANES), jnp.float32)
     norm = jnp.zeros((share, LANES), jnp.float32)
-    load.wait()
     for j in range(width // LANES):
         cols = slice(j * LANES, (j + 1) * LANES)
         w = wsum_ref[:, cols]
@@ -345,6 +362,12 @@
         mean_ref[:, cols] = new
         cross = cross + new * w
         norm = norm + new * new
+    stores = [
+        pltpu.make_async_copy(loglik, loglik_out, out_sem.at[0]),
+        pltpu.make_async_copy(mean_ref, mean_out, out_sem.at[1]),
+    ]
+    for store in stores:
+        store.start()
     cross = jnp.sum(cross, axis=1, keepdims=True)
     norm = jnp.sum(norm, axis=1, keepdims=True)
     resid = sqsum - 2.0 * cross + counts * norm + width * var_old
@@ -355,6 +378,14 @@
     )
     newvar_ref[...] = jnp.sum(jnp.where(eye, new_var, 0.0), axis=0, keepdims=True)
     newlogw_ref[...] = jnp.sum(jnp.where(eye, new_logw, 0.0), axis=0, keepdims=True)
+    last = [
+        pltpu.make_async_copy(newvar_ref, newvar_out, out_sem.at[2]),
+        pltpu.make_async_copy(newlogw_ref, newlogw_out, out_sem.at[3]),
+    ]
+    for store in last:
+        store.start()
+    for store in stores + last:
+        store.wait()
 
 
 def on_device(ncomp, npts, points, candidates, means, variances, log_weights):
@@ -368,7 +399,6 @@
     aux_rows = -(-(ncand + 1) // 8) * 8
     f32, bf16 = jnp.float32, jnp.bfloat16
     dma = pltpu.SemaphoreType.DMA
-    vmem = pl.BlockSpec(memory_space=pltpu.VMEM)
     anywhere = pl.BlockSpec(memory_space=pl.ANY)
     piece = width // pieces
     loglik, wsum, sums = pl.pallas_call(
@@ -379,7 +409,7 @@
             jax.ShapeDtypeStruct((2, owned), f32),
         ),
         in_specs=[anywhere] * 5,
-        out_specs=(vmem, vmem, vmem),
+        out_specs=(anywhere,) * 3,
         scratch_shapes=[
             pltpu.VMEM((pieces, ncomp, rows, piece), bf16),
             pltpu.VMEM((owned, width), bf16),
@@ -401,6 +431,8 @@
             pltpu.VMEM((pieces, ngroups, share, piece), f32),
             pltpu.VMEM((pieces, ngroups, share, piece), bf16),
             pltpu.VMEM((ngroups - 1, pieces, share, piece), bf16),
+            pltpu.VMEM((pieces, share, piece), f32),
+            pltpu.VMEM((2, owned), f32),
             dma((pieces + 4,)),
             dma((ny - 1, pieces)), dma((ny - 1, pieces)),
             dma((pieces,)), dma((pieces,)),
@@ -411,6 +443,7 @@
             dma((pieces,)), dma((pieces,)),
             dma((pieces,)), dma((pieces,)),
             dma((ngroups - 1, pieces)), dma((ngroups - 1, pieces)),
+            dma((pieces + 2,)),
         ],
         compiler_params=pltpu.CompilerParams(
             collective_id=0, has_side_effects=True, vmem_limit_bytes=60 * 1024 * 1024
@@ -427,9 +460,19 @@
             jax.ShapeDtypeStruct((1, share), f32),
             jax.ShapeDtypeStruct((1, share), f32),
         ),
-        in_specs=[vmem, vmem, vmem, anywhere, vmem],
-        out_specs=(vmem, vmem, vmem, vmem),
-        scratch_shapes=[pltpu.VMEM((share, width), bf16), dma],
+        in_specs=[anywhere] * 5,
+        out_specs=(anywhere,) * 4,
+        scratch_shapes=[
+            pltpu.VMEM((1, rows), f32),
+            pltpu.VMEM((share, width), f32),
+            pltpu.VMEM((2, owned), f32),
+            pltpu.VMEM((share, width), bf16),
+            pltpu.VMEM((1, owned), f32),
+            pltpu.VMEM((share, width), f32),
+            pltpu.VMEM((1, share), f32),
+            pltpu.VMEM((1, share), f32),
+            dma((5,)), dma((4,)),
+        ],
         compiler_params=pltpu.CompilerParams(vmem_limit_bytes=60 * 1024 * 1024),
         name="update",
     )(loglik, wsum, sums, means.reshape(npts, share, width), variances.reshape(1, owned))

time: 57.6 us -> 56.8 us (0.986)
  Pallas kernels: 56.7 us -> 56 us
    pallas_call x1, Pallas kernels: 2.76 us -> 2.04 us  [on_device(): pl.pallas_call(functools.partial(update_kernel, rows * ncomp * npts, owne...]
where the time goes in v7:
time: 56.8 us; the launch traced here: 56.7 us
  Pallas kernels  56 us (99%)
  between operations  0.64 us (1%)
    pallas_call x1, Pallas kernels, on_device(): pl.pallas_call(functools.partial(em_kernel, ncomp, npts, pieces), out_sha...  54 us
    pallas_call x1, Pallas kernels, on_device(): pl.pallas_call(functools.partial(update_kernel, rows * ncomp * npts, owne...  2.04 us

profile of v7, /device:TPU:0, one launch (start us, length us, event | category | flops | bytes accessed | tf_op | source)
XLA Modules:
  0.0 56.7 jit_solution(5850810149959408583)
XLA Ops:
  0.6 54.0 %em_step.1 = (f32[1,128]{1,0:T(1,128)}, f32[32,3072]{1,0:T(8,128)}, f32[2,256]{1,0:T(2,128)}) custom-call(bf16[128,3072]{1,0:T(8,128)(2,1)} %points_ref.1, s32[4,128]{1,0:T(4,128)} %bitcast.9, bf16[256,3072]{1,0:T(8,128)(2,1)} %means_ref.1, f32[1,256]{1,0:T(1,128)} %bitcast.7, f32[1,256]{1,0:T(1,128)} %bitcast.10), custom_call_target="tpu_custom_call" | custom-call | tf_op jit(solution)/shard_map/em_step/pallas_call | solution.py:404
  54.6 2.0 %update.1 = (f32[1,128]{1,0:T(1,128)}, f32[32,3072]{1,0:T(8,128)}, f32[1,32]{1,0:T(1,128)}, f32[1,32]{1,0:T(1,128)}) custom-call(f32[1,128]{1,0:T(1,128)} %get-tuple-element.11.loglik_in, f32[32,3072]{1,0:T(8,128)} %get-tuple-element.12.wsum_in, f32[2,256]{1,0:T(2,128)} %get-tuple-element.13.sums_in, bf16[8,32,3072]{2,1,0:T(8,128)(2,1)} %bitcast.6, ...), custom_call_target="tpu_custom_call" | custom-call | tf_op jit(solution)/shard_map/update/pallas_call | solution.py:455

commit v8 on v7

--- a/solution.py
+++ b/solution.py
@@ -36,8 +36,8 @@
     sibling = y * 2 + other_core
     group = here_p // 4
     bit0, bit1 = here_p % 2, (here_p // 2) % 2
-    bits = (bit0 + core * (bit1 - bit0), bit1 + core * (bit0 - bit1))
-    strides = (1 + core, 2 - core)
+    bits = (bit0 + other_core * (bit1 - bit0), bit1 + other_core * (bit0 - bit1))
+    strides = (1 + other_core, 2 - other_core)
     partners = tuple(here_p + (1 - 2 * bit) * stride for bit, stride in zip(bits, strides))
 
     barrier = pltpu.get_barrier_semaphore()
@@ -249,7 +249,7 @@
             for n in range(4):
                 lo, hi = n % 2, n // 2
                 start = (g * 4 + n) * share
-                wsend[c, lo + core * (hi - lo), hi + core * (lo - hi), g] = w[
+                wsend[c, lo + other_core * (hi - lo), hi + other_core * (lo - hi), g] = w[
                     start : start + share
                 ].astype(jnp.bfloat16)
         send(wsend.at[c, 1 - bits[0]], land0.at[c], send0.at[c], recv0.at[c],

time: 56.8 us -> 57.9 us (1.019)
  Pallas kernels: 56 us -> 57.1 us
    pallas_call x1, Pallas kernels: 54 us -> 55.1 us  [on_device(): pl.pallas_call(functools.partial(em_kernel, ncomp, npts, pieces), out_sha...]
where the time goes in v8:
time: 57.9 us; the launch traced here: 57.8 us
  Pallas kernels  57.1 us (99%)
  between operations  0.64 us (1%)
    pallas_call x1, Pallas kernels, on_device(): pl.pallas_call(functools.partial(em_kernel, ncomp, npts, pieces), out_sha...  55.1 us
    pallas_call x1, Pallas kernels, on_device(): pl.pallas_call(functools.partial(update_kernel, rows * ncomp * npts, owne...  2.04 us

profile of v8, /device:TPU:0, one launch (start us, length us, event | category | flops | bytes accessed | tf_op | source)
XLA Modules:
  0.0 57.8 jit_solution(6624749529811526158)
XLA Ops:
  0.6 55.1 %em_step.1 = (f32[1,128]{1,0:T(1,128)}, f32[32,3072]{1,0:T(8,128)}, f32[2,256]{1,0:T(2,128)}) custom-call(bf16[128,3072]{1,0:T(8,128)(2,1)} %points_ref.1, s32[4,128]{1,0:T(4,128)} %bitcast.9, bf16[256,3072]{1,0:T(8,128)(2,1)} %means_ref.1, f32[1,256]{1,0:T(1,128)} %bitcast.7, f32[1,256]{1,0:T(1,128)} %bitcast.10), custom_call_target="tpu_custom_call" | custom-call | tf_op jit(solution)/shard_map/em_step/pallas_call | solution.py:404
  55.7 2.0 %update.1 = (f32[1,128]{1,0:T(1,128)}, f32[32,3072]{1,0:T(8,128)}, f32[1,32]{1,0:T(1,128)}, f32[1,32]{1,0:T(1,128)}) custom-call(f32[1,128]{1,0:T(1,128)} %get-tuple-element.11.loglik_in, f32[32,3072]{1,0:T(8,128)} %get-tuple-element.12.wsum_in, f32[2,256]{1,0:T(2,128)} %get-tuple-element.13.sums_in, bf16[8,32,3072]{2,1,0:T(8,128)(2,1)} %bitcast.6, ...), custom_call_target="tpu_custom_call" | custom-call | tf_op jit(solution)/shard_map/update/pallas_call | solution.py:455
